TPU v7x, 32 devices: a whole 2x2x4 slice. The times are simulated.
32 devices in a mesh: dp: 16 (over z, y, x), mp: 2 (over core).
Axes of the slice: x: 2, y: 2, z: 4, core: 2. Of those that a mesh axis runs over, the one named last changes fastest.
Arguments:
- tokens_in: bfloat16 [16, 1024, 960], P('dp'), may hold values from -6 to 6
- segment_ids: int32 [16, 1024], P('dp'), may hold values from 0 to 7, never falling along the last dimension, each value on 1 to 512 neighbouring positions
- kv_owner: int32 [5], replicated, may hold values from 0 to 1, as said below
- w_query: bfloat16 [5, 960, 192], replicated, may hold values from -0.1875 to 0.1875
- w_key: bfloat16 [5, 960, 64], replicated, may hold values from -0.1875 to 0.1875
- w_value: bfloat16 [5, 960, 64], replicated, may hold values from -0.1875 to 0.1875
- w_out: bfloat16 [5, 192, 960], replicated, may hold values from -1.5 to 1.5
- attn_gain: bfloat16 [960], replicated, may hold values from 0.099609375 to 1.8984375
- w_gate: bfloat16 [960, 2560], P(None, 'mp'), may hold values from -0.1875 to 0.1875
- w_up: bfloat16 [960, 2560], P(None, 'mp'), may hold values from -0.1875 to 0.1875
- w_down: bfloat16 [2560, 960], P('mp'), may hold values from -0.125 to 0.125
- ffn_gain: bfloat16 [960], replicated, may hold values from 0.099609375 to 1.8984375
- cotangent: bfloat16 [16, 1024, 960], P('dp'), may hold values from -6 to 6
Outputs:
- tokens_out: bfloat16 [16, 1024, 960], P('dp')
- grad_in: float32 [16, 1024, 960], P('dp')
- grad_query: float32 [6, 960, 192], P('mp', 'dp')
- grad_key: float32 [6, 960, 64], P('mp', 'dp')
- grad_value: float32 [6, 960, 64], P('mp', 'dp')
- grad_out: float32 [6, 192, 960], P('mp', None, 'dp')
- grad_gate: float32 [960, 2560], P('dp', 'mp')
- grad_up: float32 [960, 2560], P('dp', 'mp')
- grad_down: float32 [2560, 960], P('mp', 'dp')
- grad_attn_gain: float32 [960], P('dp')
- grad_ffn_gain: float32 [960], P('dp')
Inputs may be any that keep to these rules, and one draw needn't show every extreme that they name: Group g is worked on by the mp device kv_owner[g]; one device holds 3 groups, the other the remaining ones.
All inputs are finite; a program needn't handle non-finite values.
Results may differ from a plain program's by a relative error of at most 0.03.
Values may be sent and summed in bfloat16 or wider, within the bound.
No kernel may reach another device: no remote copies, remote signals or barrier semaphores. Data moves between devices by JAX's collectives and lax.ppermute only.
A program may use at most 320 MiB of HBM per device.

v0:
```python
import math

import jax
import jax.numpy as jnp
from jax import lax
from jax.sharding import PartitionSpec as P

REPEAT = 2


epsilon = 1e-05
masked_value = -1e30


def rotary_tables(length, width):
    half_width = width // 2
    position = lax.broadcasted_iota(jnp.float32, (length, half_width), 0)
    column = lax.broadcasted_iota(jnp.float32, (length, half_width), 1)
    angles = position * jnp.exp(column * (-2.0 * math.log(10000.0) / width))
    return (jnp.cos(angles), jnp.sin(angles))


def rotate(values, cosine, sine_table):
    half_width = values.shape[-1] // 2
    first_half = values[..., :half_width]
    second_half = values[..., half_width:]
    cosine = cosine[:, None, :]
    sine_table = sine_table[:, None, :]
    return jnp.concatenate(
        [
            first_half * cosine - second_half * sine_table,
            second_half * cosine + first_half * sine_table,
        ],
        axis=-1,
    )


def norm_back(values, inverse, gain, grad_normed):
    scaled = grad_normed * gain
    inner_mean = jnp.mean(scaled * values, axis=-1, keepdims=True)
    return inverse * scaled - values * (inverse * inverse * inverse) * inner_mean


def per_device(
    tokens_in,
    segment_ids,
    kv_owner,
    w_query,
    w_key,
    w_value,
    w_out,
    attn_gain,
    w_gate,
    w_up,
    w_down,
    ffn_gain,
    cotangent,
):
    length = tokens_in.shape[1]
    head_size = w_key.shape[2]
    group_cols = w_query.shape[2]
    group_heads = group_cols // head_size
    group_count = kv_owner.shape[0]
    slot_count = (group_count + lax.axis_size("mp") - 1) // lax.axis_size("mp")
    column_share = w_gate.shape[1]
    score_scale = 1.0 / math.sqrt(head_size)
    block_rows = min(512, length)
    block_count = length // block_rows
    owned = kv_owner == lax.axis_index("mp")
    group_ids = jnp.arange(group_count)
    group_rank = jnp.sum(
        jnp.where((group_ids[None, :] < group_ids[:, None]) & owned[None, :], 1, 0), axis=1
    )
    selector = ((group_rank[None, :] == jnp.arange(slot_count)[:, None]) & owned[None, :]).astype(
        jnp.bfloat16
    )
    stacked = jnp.concatenate([w_query, w_key, w_value], axis=2)
    qkv_slots = jnp.einsum(
        "sg,gdc->sdc", selector, stacked, preferred_element_type=jnp.float32
    ).astype(jnp.bfloat16)
    out_slots = jnp.einsum(
        "sg,gcd->scd", selector, w_out, preferred_element_type=jnp.float32
    ).astype(jnp.bfloat16)
    gate_up = jnp.concatenate([w_gate, w_up], axis=1)
    cosine, sine_table = rotary_tables(length, head_size)
    segment_row = segment_ids[0]
    positions = jnp.arange(length)
    starts = jnp.arange(block_count) * block_rows

    def attend_block(start, queries, keys_all):
        query_block = lax.dynamic_slice_in_dim(queries, start, block_rows, 1)
        query_block = query_block.reshape(slot_count, block_rows, group_heads, head_size)
        segment_block = lax.dynamic_slice_in_dim(segment_row, start, block_rows, 0)
        query_positions = start + jnp.arange(block_rows)
        allowed = (segment_block[:, None] == segment_row[None, :]) & (
            positions[None, :] <= query_positions[:, None]
        )
        scores = (
            jnp.einsum("sqjc,skc->sjqk", query_block, keys_all, preferred_element_type=jnp.float32)
            * score_scale
        )
        scores = jnp.where(allowed[None, None], scores, masked_value)
        row_max = jnp.max(scores, axis=-1, keepdims=True)
        exponent = jnp.exp(scores - row_max)
        probabilities = exponent / jnp.sum(exponent, axis=-1, keepdims=True)
        return (query_block, probabilities)

    hidden = tokens_in[0].astype(jnp.float32)
    inputs = []
    saved_all = []
    for repeat_index in range(REPEAT):
        inputs.append(hidden)
        forward_inverse_one = lax.rsqrt(jnp.mean(hidden * hidden, axis=-1, keepdims=True) + epsilon)
        forward_normed = (hidden * forward_inverse_one * attn_gain).astype(jnp.bfloat16)
        projected = jnp.einsum(
            "ld,sdc->slc", forward_normed, qkv_slots, preferred_element_type=jnp.float32
        )
        query_pre = projected[..., :group_cols].reshape(slot_count, length, group_heads, head_size)
        key_pre = projected[..., group_cols : group_cols + head_size][:, :, None, :]
        forward_queries = (
            rotate(query_pre, cosine, sine_table)
            .reshape(slot_count, length, group_cols)
            .astype(jnp.bfloat16)
        )
        forward_keys_all = rotate(key_pre, cosine, sine_table)[:, :, 0, :].astype(jnp.bfloat16)
        forward_values_all = projected[..., group_cols + head_size :].astype(jnp.bfloat16)

        def forward_one_block(start):
            query_block, probabilities = attend_block(start, forward_queries, forward_keys_all)
            piece = jnp.einsum(
                "sjqk,skc->sqjc",
                probabilities.astype(jnp.bfloat16),
                forward_values_all,
                preferred_element_type=jnp.float32,
            )
            return piece.astype(jnp.bfloat16).reshape(slot_count, block_rows, group_cols)

        pieces = lax.map(forward_one_block, starts)
        forward_attended = jnp.moveaxis(pieces, 0, 1).reshape(slot_count, length, group_cols)
        partial_sum = jnp.einsum(
            "slc,scd->ld", forward_attended, out_slots, preferred_element_type=jnp.float32
        )
        branch = lax.psum(
            partial_sum.astype(jnp.bfloat16).astype(jnp.float32).astype(jnp.bfloat16), "mp"
        ).astype(jnp.float32)
        forward_middle = hidden + branch
        forward_inverse_two = lax.rsqrt(
            jnp.mean(forward_middle * forward_middle, axis=-1, keepdims=True) + epsilon
        )
        forward_normed_two = (forward_middle * forward_inverse_two * ffn_gain).astype(jnp.bfloat16)
        forward_gate_pre = jnp.dot(forward_normed_two, gate_up, preferred_element_type=jnp.float32)
        forward_inner = (
            jax.nn.silu(forward_gate_pre[:, :column_share]) * forward_gate_pre[:, column_share:]
        ).astype(jnp.bfloat16)
        partial_two = jnp.dot(forward_inner, w_down, preferred_element_type=jnp.float32)
        branch_two = lax.psum(
            partial_two.astype(jnp.bfloat16).astype(jnp.float32).astype(jnp.bfloat16), "mp"
        ).astype(jnp.float32)
        forward_saved = (
            hidden,
            forward_inverse_one,
            forward_normed,
            forward_queries,
            forward_keys_all,
            forward_values_all,
            forward_attended,
            forward_middle,
            forward_inverse_two,
            forward_normed_two,
            forward_gate_pre,
            forward_inner,
        )
        hidden = forward_middle + branch_two
        saved = forward_saved
        saved_all.append(saved)
    grad_hidden = cotangent[0].astype(jnp.float32)
    totals = None
    reduced = None
    for repeat_index in reversed(range(REPEAT)):
        saved = saved_all[repeat_index]
        grad_out = grad_hidden
        (
            backward_hidden,
            inverse_one,
            normed,
            backward_queries,
            backward_keys_all,
            values_all,
            attended,
            middle,
            inverse_two,
            normed_two,
            gate_pre,
            inner,
        ) = saved
        ffn_grad = grad_out.astype(jnp.bfloat16)
        grad_inner = jnp.einsum("ld,fd->lf", ffn_grad, w_down, preferred_element_type=jnp.float32)
        gate_value = gate_pre[:, :column_share]
        lift_value = gate_pre[:, column_share:]
        sigmoid = jax.nn.sigmoid(gate_value)
        grad_gate = grad_inner * lift_value * sigmoid * (1.0 + gate_value * (1.0 - sigmoid))
        grad_lift = grad_inner * gate_value * sigmoid
        grad_gate_up = jnp.concatenate([grad_gate, grad_lift], axis=1).astype(jnp.bfloat16)
        grad_normed_two = lax.psum(
            jnp.einsum(
                "lf,df->ld", grad_gate_up, gate_up, preferred_element_type=jnp.float32
            ).astype(jnp.bfloat16),
            "mp",
        ).astype(jnp.float32)
        backward_d_gate_up = jnp.einsum(
            "ld,lf->df", normed_two, grad_gate_up, preferred_element_type=jnp.float32
        )
        backward_d_down = jnp.einsum(
            "lf,ld->fd", inner, ffn_grad, preferred_element_type=jnp.float32
        )
        backward_d_ffn_gain = jnp.sum(grad_normed_two * middle * inverse_two, axis=0)
        grad_middle = grad_out + norm_back(middle, inverse_two, ffn_gain, grad_normed_two)
        attn_grad = grad_middle.astype(jnp.bfloat16)
        grad_attended = jnp.einsum(
            "ld,scd->slc", attn_grad, out_slots, preferred_element_type=jnp.float32
        ).astype(jnp.bfloat16)
        backward_d_out = jnp.einsum(
            "slc,ld->scd", attended, attn_grad, preferred_element_type=jnp.float32
        )

        def backward_one_block(carry, start):
            grad_keys, grad_values = carry
            query_block, probabilities = attend_block(start, backward_queries, backward_keys_all)
            grad_block = lax.dynamic_slice_in_dim(grad_attended, start, block_rows, 1)
            grad_block = grad_block.reshape(slot_count, block_rows, group_heads, head_size)
            grad_probs = jnp.einsum(
                "sqjc,skc->sjqk", grad_block, values_all, preferred_element_type=jnp.float32
            )
            delta = jnp.sum(probabilities * grad_probs, axis=-1, keepdims=True)
            grad_scores = (probabilities * (grad_probs - delta)).astype(jnp.bfloat16)
            grad_query = (
                jnp.einsum(
                    "sjqk,skc->sqjc",
                    grad_scores,
                    backward_keys_all,
                    preferred_element_type=jnp.float32,
                )
                * score_scale
            )
            grad_keys = (
                grad_keys
                + jnp.einsum(
                    "sjqk,sqjc->skc", grad_scores, query_block, preferred_element_type=jnp.float32
                )
                * score_scale
            )
            grad_values = grad_values + jnp.einsum(
                "sjqk,sqjc->skc",
                probabilities.astype(jnp.bfloat16),
                grad_block,
                preferred_element_type=jnp.float32,
            )
            return ((grad_keys, grad_values), grad_query)

        zero_state = jnp.zeros((slot_count, length, head_size), jnp.float32)
        (grad_keys, grad_values), grad_pieces = lax.scan(
            backward_one_block, (zero_state, zero_state), starts
        )
        grad_queries = jnp.moveaxis(grad_pieces, 0, 1).reshape(
            slot_count, length, group_heads, head_size
        )
        grad_query_pre = rotate(grad_queries, cosine, -sine_table).reshape(
            slot_count, length, group_cols
        )
        grad_key_pre = rotate(grad_keys[:, :, None, :], cosine, -sine_table)[:, :, 0, :]
        grad_projected = jnp.concatenate(
            [grad_query_pre, grad_key_pre, grad_values], axis=2
        ).astype(jnp.bfloat16)
        grad_normed = lax.psum(
            jnp.einsum(
                "slc,sdc->ld", grad_projected, qkv_slots, preferred_element_type=jnp.float32
            ).astype(jnp.bfloat16),
            "mp",
        ).astype(jnp.float32)
        backward_d_qkv = jnp.einsum(
            "ld,slc->sdc", normed, grad_projected, preferred_element_type=jnp.float32
        )
        backward_d_attn_gain = jnp.sum(grad_normed * backward_hidden * inverse_one, axis=0)
        backward_grad_hidden = grad_middle + norm_back(
            backward_hidden, inverse_one, attn_gain, grad_normed
        )
        grad_hidden = backward_grad_hidden
        grads = (
            backward_d_qkv,
            backward_d_out,
            backward_d_gate_up,
            backward_d_down,
            backward_d_attn_gain,
            backward_d_ffn_gain,
        )
        totals = grads if totals is None else jax.tree.map(jnp.add, totals, grads)
    d_qkv, d_out, d_gate_up, d_down, d_attn_gain, d_ffn_gain = totals
    part_query = d_qkv[..., :group_cols]
    part_key = d_qkv[..., group_cols : group_cols + head_size]
    part_value = d_qkv[..., group_cols + head_size :]
    part_gate = d_gate_up[:, :column_share]
    part_up = d_gate_up[:, column_share:]
    reduced = (
        lax.psum_scatter(part_query, "dp", scatter_dimension=1, tiled=True),
        lax.psum_scatter(part_key, "dp", scatter_dimension=1, tiled=True),
        lax.psum_scatter(part_value, "dp", scatter_dimension=1, tiled=True),
        lax.psum_scatter(d_out, "dp", scatter_dimension=2, tiled=True),
        lax.psum_scatter(part_gate, "dp", scatter_dimension=0, tiled=True),
        lax.psum_scatter(part_up, "dp", scatter_dimension=0, tiled=True),
        lax.psum_scatter(d_down, "dp", scatter_dimension=1, tiled=True),
        lax.psum_scatter(d_attn_gain, "dp", scatter_dimension=0, tiled=True),
        lax.psum_scatter(d_ffn_gain, "dp", scatter_dimension=0, tiled=True),
    )
    return (
        hidden.astype(jnp.bfloat16)[None],
        grad_hidden[None],
        reduced[0],
        reduced[1],
        reduced[2],
        reduced[3],
        reduced[4],
        reduced[5],
        reduced[6],
        reduced[7],
        reduced[8],
    )


def solution(mesh):
    in_specs = (
        P("dp", None, None),
        P("dp", None),
        P(),
        P(),
        P(),
        P(),
        P(),
        P(),
        P(None, "mp"),
        P(None, "mp"),
        P("mp", None),
        P(),
        P("dp", None, None),
    )
    out_specs = (
        P("dp", None, None),
        P("dp", None, None),
        P("mp", "dp", None),
        P("mp", "dp", None),
        P("mp", "dp", None),
        P("mp", None, "dp"),
        P("dp", "mp"),
        P("dp", "mp"),
        P("mp", "dp"),
        P("dp"),
        P("dp"),
    )
    return jax.shard_map(
        per_device, mesh=mesh, in_specs=in_specs, out_specs=out_specs, check_vma=False
    )
```

profile of v0, /device:TPU:0, one launch (start us, length us, event | category | flops | bytes accessed | tf_op | source)
XLA Modules:
  0.0 1243.7 jit_solution(517745990724526521)
XLA Ops:
  26.2 52.2 %while.52 = (s32[]{:T(128)}, bf16[2,3,512,192]{2,3,1,0:T(8,128)(2,1)}, s32[2]{0:T(128)S(1)}, s32[1024]{0:T(1024)S(1)}, s32[1,1024]{1,0:T(1,128)S(1)}, /*index=5*...) while((s32[]{:T(128)}, ...), condition=%wide.region_5.6_spmd.clone, body=%wide.region_2.5_spmd.clone.sunk | while | flops 1238140416 | bytes 43174568 | solution.py:138
  32.2 11.0 fusion.394
  58.2 11.0 fusion.394
  93.2 18.6 %all-reduce.25.cloned.1.call-done = bf16[1024,960]{0,1:T(8,128)(2,1)} async-done(((bf16[1024,960]{0,1:T(8,128)(2,1)}), bf16[1024,960]{0,1:T(8,128)(2,1)}) %all-reduce.25.cloned.1.call-update) | async-done | bytes 1966096 | tf_op jit(solution)/shard_map/psum | solution.py:143
  133.8 21.9 %all-reduce.27.cloned.1.call-done = bf16[1024,960]{0,1:T(8,128)(2,1)} async-done(((bf16[1024,960]{0,1:T(8,128)(2,1)}), bf16[1024,960]{0,1:T(8,128)(2,1)}) %all-reduce.27.cloned.1.call-update) | async-done | bytes 1966096 | tf_op jit(solution)/shard_map/psum | solution.py:156
  168.2 52.0 %while.53 = (s32[]{:T(128)}, bf16[2,3,512,192]{2,3,1,0:T(8,128)(2,1)}, s32[2]{0:T(128)S(1)}, s32[1024]{0:T(1024)S(1)}, s32[1,1024]{1,0:T(1,128)S(1)}, /*index=5*...) while((s32[]{:T(128)}, ...), condition=%wide.region_13.14_spmd.clone, body=%wide.region_10.13_spmd.clone.sunk | while | flops 1238140416 | bytes 43174568 | solution.py:138
  174.2 11.0 fusion.400
  200.2 11.0 fusion.400
  227.5 22.1 %all-reduce.29.cloned.1.call-done = bf16[1024,960]{0,1:T(8,128)(2,1)} async-done(((bf16[1024,960]{0,1:T(8,128)(2,1)}), bf16[1024,960]{0,1:T(8,128)(2,1)}) %all-reduce.29.cloned.1.call-update) | async-done | bytes 1966096 | tf_op jit(solution)/shard_map/psum | solution.py:143
  281.4 22.3 %all-reduce.31.cloned.1.call-done = bf16[1024,960]{0,1:T(8,128)(2,1)} async-done(((bf16[1024,960]{0,1:T(8,128)(2,1)}), bf16[1024,960]{0,1:T(8,128)(2,1)}) %all-reduce.31.cloned.1.call-update) | async-done | bytes 1966096 | tf_op jit(solution)/shard_map/psum | solution.py:204
  315.8 133.1 %while.54 = (s32[]{:T(128)}, f32[3,1024,64]{1,2,0:T(8,128)}, f32[3,1024,64]{1,2,0:T(8,128)}, f32[2,3,512,3,64]{2,4,3,1,0:T(8,128)}, s32[2]{0:T(128)S(1)}, /*inde...) while((s32[]{:T(128)}, f32[3,1024,64]{1,2,0:T(8,128)}, ...), condition=%wide.region_23.24_spmd.clone, body=%wide.region_19.23_spmd.clone.sunk | while | flops 3702229504 | bytes 173337328 | solution.py:261
  334.4 12.2 fusion.416
  346.6 12.7 %fusion.417 = bf16[3,3,512,1024]{3,2,1,0:T(8,128)(2,1)S(1)} fusion(f32[3,512,3,1024]{3,1,2,0:T(8,128)} %get-tuple-element.813, f32[3,3,512]{2,1,0:T(4,128)S(1)} %get-tuple-element.814, f32[3,3,512,1024]{3,2,1,0:T(8,128)} %get-tuple-element.810, f32[3,3,512]{2,1,0:T(4,128)S(1)} %get-tuple-element.811), kind=kLoop, calls=%fused_computation.57.clone.1 | loop fusion | flops 18874368 | bytes 47222784 | tf_op jit(solution)/shard_map/while/body/eval_jaxpr/convert_element_type | solution.py:235
  400.5 12.2 fusion.416
  412.6 12.7 %fusion.417 = bf16[3,3,512,1024]{3,2,1,0:T(8,128)(2,1)S(1)} fusion(f32[3,512,3,1024]{3,1,2,0:T(8,128)} %get-tuple-element.813, f32[3,3,512]{2,1,0:T(4,128)S(1)} %get-tuple-element.814, f32[3,3,512,1024]{3,2,1,0:T(8,128)} %get-tuple-element.810, f32[3,3,512]{2,1,0:T(4,128)S(1)} %get-tuple-element.811), kind=kLoop, calls=%fused_computation.57.clone.1 | loop fusion | flops 18874368 | bytes 47222784 | tf_op jit(solution)/shard_map/while/body/eval_jaxpr/convert_element_type | solution.py:235
  463.2 16.6 %all-reduce.33.cloned.1.call-done = bf16[1024,960]{0,1:T(8,128)(2,1)} async-done(((bf16[1024,960]{0,1:T(8,128)(2,1)}), bf16[1024,960]{0,1:T(8,128)(2,1)}) %all-reduce.33.cloned.1.call-update) | async-done | bytes 1966096 | tf_op jit(solution)/shard_map/psum | solution.py:274
  544.3 133.0 %while.55 = (s32[]{:T(128)}, f32[3,1024,64]{1,2,0:T(8,128)}, f32[3,1024,64]{1,2,0:T(8,128)}, f32[2,3,512,3,64]{2,4,3,1,0:T(8,128)}, s32[2]{0:T(128)S(1)}, /*inde...) while((s32[]{:T(128)}, f32[3,1024,64]{1,2,0:T(8,128)}, ...), condition=%wide.region_32.33_spmd.clone, body=%wide.region_28.32_spmd.clone.sunk | while | flops 3702229504 | bytes 173337328 | solution.py:261
  562.8 12.2 fusion.435
  574.9 12.7 %fusion.436 = bf16[3,3,512,1024]{3,2,1,0:T(8,128)(2,1)S(1)} fusion(f32[3,512,3,1024]{3,1,2,0:T(8,128)} %get-tuple-element.830, f32[3,3,512]{2,1,0:T(4,128)S(1)} %get-tuple-element.831, f32[3,3,512,1024]{3,2,1,0:T(8,128)} %get-tuple-element.827, f32[3,3,512]{2,1,0:T(4,128)S(1)} %get-tuple-element.828), kind=kLoop, calls=%fused_computation.96.clone.1 | loop fusion | flops 18874368 | bytes 47222784 | tf_op jit(solution)/shard_map/while/body/eval_jaxpr/convert_element_type | solution.py:235
  628.8 12.2 fusion.435
  641.0 12.7 %fusion.436 = bf16[3,3,512,1024]{3,2,1,0:T(8,128)(2,1)S(1)} fusion(f32[3,512,3,1024]{3,1,2,0:T(8,128)} %get-tuple-element.830, f32[3,3,512]{2,1,0:T(4,128)S(1)} %get-tuple-element.831, f32[3,3,512,1024]{3,2,1,0:T(8,128)} %get-tuple-element.827, f32[3,3,512]{2,1,0:T(4,128)S(1)} %get-tuple-element.828), kind=kLoop, calls=%fused_computation.96.clone.1 | loop fusion | flops 18874368 | bytes 47222784 | tf_op jit(solution)/shard_map/while/body/eval_jaxpr/convert_element_type | solution.py:235
  686.5 12.0 convolution_add_fusion
  734.0 398.0 %fusion.270 = (f32[64,1280]{1,0:T(8,128)S(1)}, f32[64,1280]{1,0:T(8,128)S(1)}, f32[1280,64]{0,1:T(8,128)S(1)}) fusion(f32[960,1280]{1,0:T(8,128)} %get-tuple-element.532, f32[960,1280]{1,0:T(8,128)} %get-tuple-element.531, f32[1280,960]{0,1:T(8,128)} %convolution_add_fusion.1), kind=kCustom, calls=%all-reduce-scatter.3 | all-reduce-scatter fusion | flops 3932161 | bytes 15729152
  1168.1 51.6 %all-reduce.12 = (f32[960]{0:T(1024)S(1)}, f32[960]{0:T(1024)S(1)}) all-reduce(f32[960]{0:T(1024)S(1)} %add.273, f32[960]{0:T(1024)S(1)} %add.274), channel_id=9, replica_groups=mesh['dp'=16,'mp'=2] {'dp'}, use_global_device_ids=true, to_apply=%region_44.45.clone | all-reduce | flops 1920 | bytes 15360
  (409 shorter events, 503.2 us)
Async XLA Ops:
  7.2 122.3 %copy-start = (bf16[1280,960]{0,1:T(8,128)(2,1)S(1)}, bf16[1280,960]{0,1:T(8,128)(2,1)}, u32[]{:S(2)}) copy-start(bf16[1280,960]{0,1:T(8,128)(2,1)} %param.31) | copy-start | bytes 7372804
  7.2 104.6 %all-reduce.25.cloned.1.call-start = ((), (), s32[]{:S(2)}) async-start(), calls=%async_computation | async-start | bytes 3932160 | tf_op jit(solution)/shard_map/psum | solution.py:143
  26.2 53.8 %copy-start.86 = (pred[5]{0:T(512)(128)(4,1)S(1)}, pred[5]{0:T(512)(128)(4,1)}, u32[]{:S(2)}) copy-start(pred[5]{0:T(512)(128)(4,1)} %copy-done.85) | copy-start | bytes 19
  26.2 53.8 %copy-start.88 = (s32[5]{0:T(128)S(1)}, s32[5]{0:T(128)}, u32[]{:S(2)}) copy-start(s32[5]{0:T(128)} %copy-done.87) | copy-start | bytes 64
  87.9 67.8 %all-reduce.27.cloned.1.call-start = ((), (), s32[]{:S(2)}) async-start(), calls=%async_computation.1 | async-start | bytes 3932160 | tf_op jit(solution)/shard_map/psum | solution.py:156
  88.0 27.6 %copy-start.55 = (f32[960]{0:T(1024)}, f32[960]{0:T(1024)S(1)}, u32[]{:S(2)}) copy-start(f32[960]{0:T(1024)S(1)} %convert_element_type.189) | copy-start | bytes 11524
  133.4 116.3 %all-reduce.29.cloned.1.call-start = ((), (), s32[]{:S(2)}) async-start(), calls=%async_computation.2 | async-start | bytes 3932160 | tf_op jit(solution)/shard_map/psum | solution.py:143
  133.8 27.9 %copy-start.60 = (f32[960]{0:T(1024)S(1)}, f32[960]{0:T(1024)}, u32[]{:S(2)}) copy-start(f32[960]{0:T(1024)} %copy-done.59) | copy-start | bytes 11524
  227.3 27.7 %copy-start.56 = (f32[960]{0:T(1024)S(1)}, f32[960]{0:T(1024)}, u32[]{:S(2)}) copy-start(f32[960]{0:T(1024)} %copy-done.55) | copy-start | bytes 11524
  227.3 76.4 %all-reduce.31.cloned.1.call-start = ((), (), s32[]{:S(2)}) async-start(), calls=%async_computation.3 | async-start | bytes 3932160 | tf_op jit(solution)/shard_map/psum | solution.py:204
  253.2 55.3 %copy-start.63 = (f32[1024]{0:T(1024)}, f32[1024]{0:T(1024)S(1)}, u32[]{:S(2)}) copy-start(f32[1024]{0:T(1024)S(1)} %get-tuple-element.558) | copy-start | bytes 12292
  253.2 55.3 %copy-start.65 = (f32[1024]{0:T(1024)}, f32[1024]{0:T(1024)S(1)}, u32[]{:S(2)}) copy-start(f32[1024]{0:T(1024)S(1)} %get-tuple-element.557) | copy-start | bytes 12292
  281.3 198.4 %all-reduce.33.cloned.1.call-start = ((), (), s32[]{:S(2)}) async-start(), calls=%async_computation.4 | async-start | bytes 3932160 | tf_op jit(solution)/shard_map/psum | solution.py:274
  457.4 73.8 %all-reduce.35.cloned.1.call-start = ((), (), s32[]{:S(2)}) async-start(), calls=%async_computation.5 | async-start | bytes 3932160 | tf_op jit(solution)/shard_map/psum | solution.py:204
  457.5 22.3 %copy-start.61 = (f32[960]{0:T(1024)S(1)}, f32[960]{0:T(1024)}, u32[]{:S(2)}) copy-start(f32[960]{0:T(1024)} %copy-done.59) | copy-start | bytes 11524
  508.8 655.4 %all-reduce.39.cloned.1.call-start = ((), (), s32[]{:S(2)}) async-start(), calls=%async_computation.7 | async-start | bytes 7864320 | tf_op jit(solution)/shard_map/psum | solution.py:156
  685.9 544.5 %all-reduce.37.cloned.1.call-start = ((), (), s32[]{:S(2)}) async-start(), calls=%async_computation.6 | async-start | bytes 16908288
  734.0 410.3 %copy-start.84 = (u32[32]{0:T(128)S(1)}, u32[32]{0:T(128)}, u32[]{:S(2)}) copy-start(u32[32]{0:T(128)} %constant.114) | copy-start | bytes 388
  1132.0 32.3 %copy-start.78 = (f32[960]{0:T(1024)S(1)}, f32[960]{0:T(1024)}, u32[]{:S(2)}) copy-start(f32[960]{0:T(1024)} %get-tuple-element.410) | copy-start | bytes 11524
  1132.0 32.3 %copy-start.80 = (f32[960]{0:T(1024)S(1)}, f32[960]{0:T(1024)}, u32[]{:S(2)}) copy-start(f32[960]{0:T(1024)} %get-tuple-element.408) | copy-start | bytes 11524
  1132.8 13.5 %collective-permute-start.2 = (f32[1280,60]{0,1:T(8,128)}, f32[1280,60]{0,1:T(8,128)}, u32[]{:S(2)}, u32[]{:S(2)}) collective-permute-start(f32[1280,60]{0,1:T(8,128)} %slice.163), channel_id=1, source_target_pairs={{0,2},{2,4},{4,6},{6,8},{8,10},{10,12},{12,14},{14,16},{16,18},{18... | collective-permute-start | bytes 921608
  1138.6 13.9 %collective-permute-start.1 = (f32[60,1280]{1,0:T(8,128)}, f32[60,1280]{1,0:T(8,128)}, u32[]{:S(2)}, u32[]{:S(2)}) collective-permute-start(f32[60,1280]{1,0:T(8,128)} %slice.162), channel_id=1, source_target_pairs={{0,2},{2,4},{4,6},{6,8},{8,10},{10,12},{12,14},{14,16},{16,18},{18... | collective-permute-start | bytes 921608
  1141.9 16.8 %collective-permute-start = (f32[60,1280]{1,0:T(8,128)}, f32[60,1280]{1,0:T(8,128)}, u32[]{:S(2)}, u32[]{:S(2)}) collective-permute-start(f32[60,1280]{1,0:T(8,128)} %slice.161), channel_id=1, source_target_pairs={{0,2},{2,4},{4,6},{6,8},{8,10},{10,12},{12,14},{14,16},{16,18},{18... | collective-permute-start | bytes 921608
  1155.7 65.1 %copy-start.81 = (f32[1024]{0:T(1024)S(1)}, f32[1024]{0:T(1024)}, u32[]{:S(2)}) copy-start(f32[1024]{0:T(1024)} %get-tuple-element.551) | copy-start | bytes 12292
  (88 other events, 460.5 us)
Sparse Core Ops, SparseCore 0:
  88.0 23.7 all-reduce.24
  133.5 22.1 all-reduce.26
  227.4 22.1 all-reduce.28
  281.5 22.1 all-reduce.30
  457.5 22.1 all-reduce.32
  509.0 22.1 all-reduce.34
  686.0 25.9 all-reduce.38
  734.1 406.5 all-reduce.36
where the time goes:
time: 1250 us; the launch traced here: 1240 us
  blocking collectives  450 us (36%)
  matrix products  390 us (31%)
  other arithmetic  131 us (10%)
  local copies, waits for them, and re-layouts  118 us (9%)
  waiting for transfers between devices  110 us (9%)
  between operations  17.2 us (1%)
  loops' own time  16.8 us (1%)
    unnamed x2, blocking collectives  450 us
    sub x8, matrix products, attend_block(): exponent = jnp.exp(scores - row_max)  87.8 us
    convert_element_type x4, other arithmetic, backward_one_block(): grad_scores = (probabilities * (grad_probs - delta)).astype(jnp.bfloat16)  50.7 us
    dot_general x4, matrix products, backward_one_block(): jnp.einsum('sqjc,skc->sjqk', grad_block, values_all, preferred_element_ty...  48.7 us
    unnamed x216, local copies, waits for them, and re-layouts  47.9 us
    psum x2, waiting for transfers between devices, per_device(): lax.psum(partial_sum.astype(jnp.bfloat16).astype(jnp.float32).astype(jnp....  40.7 us
    dot_general x4, matrix products, backward_one_block(): jnp.einsum('sjqk,sqjc->skc', probabilities.astype(jnp.bfloat16), grad_blo...  36.3 us
    dot_general x4, matrix products, forward_one_block(): jnp.einsum('sjqk,skc->sqjc', probabilities.astype(jnp.bfloat16), forward_...  32.5 us
  transfers between devices with their start and end apart: 11, of which 8 were waited for; matrix products, arithmetic and copies ran while one was open for 40% of the time, Pallas kernels for 0%

commit v1 on v0

--- a/solution.py
+++ b/solution.py
@@ -39,6 +39,75 @@
     scaled = grad_normed * gain
     inner_mean = jnp.mean(scaled * values, axis=-1, keepdims=True)
     return inverse * scaled - values * (inverse * inverse * inverse) * inner_mean
+
+
+def sum_over_mp(partial_sum):
+    own = partial_sum.astype(jnp.bfloat16)
+    other = lax.ppermute(own, "mp", [(0, 1), (1, 0)])
+    return own.astype(jnp.float32) + other.astype(jnp.float32)
+
+
+def stage_plans(bit_count):
+    if bit_count < 4:
+        return [[[bit] for bit in range(bit_count)]] * 3
+    rest = list(range(4, bit_count))
+    tail = [[bit] for bit in rest]
+    return [
+        [[0], [1], [2, 3]] + tail,
+        [[1], [0], [2, 3]] + tail,
+        [[2], [0], [1], [3]] + tail,
+    ]
+
+
+def shard_order(plan):
+    bits = [bit for stage in plan for bit in stage]
+    order = []
+    for place in range(1 << len(bits)):
+        shard = 0
+        for rank, bit in enumerate(bits):
+            if place >> (len(bits) - 1 - rank) & 1:
+                shard |= 1 << bit
+        order.append(shard)
+    return order
+
+
+def reduce_stage(current, stage, last):
+    size = lax.axis_size("dp")
+    index = lax.axis_index("dp")
+    mine = 0
+    for bit in stage:
+        mine = mine * 2 + ((index >> bit) & 1)
+    ways = 1 << len(stage)
+    pieces = current.shape[0] // ways
+    total = lax.dynamic_slice_in_dim(current, mine * pieces, pieces, 0).astype(jnp.float32)
+    received = []
+    for offset in range(1, ways):
+        mask = 0
+        for rank, bit in enumerate(stage):
+            if offset >> (len(stage) - 1 - rank) & 1:
+                mask |= 1 << bit
+        outgoing = lax.dynamic_slice_in_dim(current, (mine ^ offset) * pieces, pieces, 0)
+        received.append(lax.ppermute(outgoing, "dp", [(i, i ^ mask) for i in range(size)]))
+    for piece in received:
+        total = total + piece.astype(jnp.float32)
+    return total if last else total.astype(jnp.bfloat16)
+
+
+def reduce_scatter(payload, plan):
+    for number, stage in enumerate(plan):
+        payload = reduce_stage(payload, stage, number == len(plan) - 1)
+    return payload[0]
+
+
+def to_payload(grad, plan, extra=None):
+    size = lax.axis_size("dp")
+    rows = grad.shape[0] // size
+    padded = -(-(rows + 1) // 16) * 16
+    shards = grad.astype(jnp.bfloat16).reshape(size, rows, grad.shape[1])
+    if extra is None:
+        extra = jnp.zeros((size, padded - rows, grad.shape[1]), jnp.bfloat16)
+    shards = jnp.concatenate([shards, extra], axis=1)
+    return jnp.stack([shards[shard] for shard in shard_order(plan)])
 
 
 def per_device(
@@ -140,9 +209,7 @@
         partial_sum = jnp.einsum(
             "slc,scd->ld", forward_attended, out_slots, preferred_element_type=jnp.float32
         )
-        branch = lax.psum(
-            partial_sum.astype(jnp.bfloat16).astype(jnp.float32).astype(jnp.bfloat16), "mp"
-        ).astype(jnp.float32)
+        branch = sum_over_mp(partial_sum)
         forward_middle = hidden + branch
         forward_inverse_two = lax.rsqrt(
             jnp.mean(forward_middle * forward_middle, axis=-1, keepdims=True) + epsilon
@@ -153,9 +220,7 @@
             jax.nn.silu(forward_gate_pre[:, :column_share]) * forward_gate_pre[:, column_share:]
         ).astype(jnp.bfloat16)
         partial_two = jnp.dot(forward_inner, w_down, preferred_element_type=jnp.float32)
-        branch_two = lax.psum(
-            partial_two.astype(jnp.bfloat16).astype(jnp.float32).astype(jnp.bfloat16), "mp"
-        ).astype(jnp.float32)
+        branch_two = sum_over_mp(partial_two)
         forward_saved = (
             hidden,
             forward_inverse_one,
@@ -201,17 +266,14 @@
         grad_gate = grad_inner * lift_value * sigmoid * (1.0 + gate_value * (1.0 - sigmoid))
         grad_lift = grad_inner * gate_value * sigmoid
         grad_gate_up = jnp.concatenate([grad_gate, grad_lift], axis=1).astype(jnp.bfloat16)
-        grad_normed_two = lax.psum(
-            jnp.einsum(
-                "lf,df->ld", grad_gate_up, gate_up, preferred_element_type=jnp.float32
-            ).astype(jnp.bfloat16),
-            "mp",
-        ).astype(jnp.float32)
+        grad_normed_two = sum_over_mp(
+            jnp.einsum("lf,df->ld", grad_gate_up, gate_up, preferred_element_type=jnp.float32)
+        )
         backward_d_gate_up = jnp.einsum(
             "ld,lf->df", normed_two, grad_gate_up, preferred_element_type=jnp.float32
         )
         backward_d_down = jnp.einsum(
-            "lf,ld->fd", inner, ffn_grad, preferred_element_type=jnp.float32
+            "ld,lf->df", ffn_grad, inner, preferred_element_type=jnp.float32
         )
         backward_d_ffn_gain = jnp.sum(grad_normed_two * middle * inverse_two, axis=0)
         grad_middle = grad_out + norm_back(middle, inverse_two, ffn_gain, grad_normed_two)
@@ -220,8 +282,8 @@
             "ld,scd->slc", attn_grad, out_slots, preferred_element_type=jnp.float32
         ).astype(jnp.bfloat16)
         backward_d_out = jnp.einsum(
-            "slc,ld->scd", attended, attn_grad, preferred_element_type=jnp.float32
-        )
+            "ld,slc->dsc", attn_grad, attended, preferred_element_type=jnp.float32
+        ).reshape(attn_grad.shape[1], slot_count * group_cols)
 
         def backward_one_block(carry, start):
             grad_keys, grad_values = carry
@@ -271,12 +333,9 @@
         grad_projected = jnp.concatenate(
             [grad_query_pre, grad_key_pre, grad_values], axis=2
         ).astype(jnp.bfloat16)
-        grad_normed = lax.psum(
-            jnp.einsum(
-                "slc,sdc->ld", grad_projected, qkv_slots, preferred_element_type=jnp.float32
-            ).astype(jnp.bfloat16),
-            "mp",
-        ).astype(jnp.float32)
+        grad_normed = sum_over_mp(
+            jnp.einsum("slc,sdc->ld", grad_projected, qkv_slots, preferred_element_type=jnp.float32)
+        )
         backward_d_qkv = jnp.einsum(
             "ld,slc->sdc", normed, grad_projected, preferred_element_type=jnp.float32
         )
@@ -295,21 +354,35 @@
         )
         totals = grads if totals is None else jax.tree.map(jnp.add, totals, grads)
     d_qkv, d_out, d_gate_up, d_down, d_attn_gain, d_ffn_gain = totals
-    part_query = d_qkv[..., :group_cols]
-    part_key = d_qkv[..., group_cols : group_cols + head_size]
-    part_value = d_qkv[..., group_cols + head_size :]
-    part_gate = d_gate_up[:, :column_share]
-    part_up = d_gate_up[:, column_share:]
+    size = lax.axis_size("dp")
+    features = d_attn_gain.shape[0]
+    rows = features // size
+    plans = stage_plans(size.bit_length() - 1)
+    extra_rows = -(-(rows + 1) // 16) * 16 - rows
+    gains = jnp.zeros((size, extra_rows, column_share), jnp.float32)
+    gains = gains.at[:, 0, :rows].set(d_attn_gain.reshape(size, rows))
+    gains = gains.at[:, 0, rows : 2 * rows].set(d_ffn_gain.reshape(size, rows))
+    gains = gains.astype(jnp.bfloat16)
+    gate_total = reduce_scatter(
+        to_payload(d_gate_up[:, :column_share], plans[0], gains), plans[0]
+    )
+    up_total = reduce_scatter(to_payload(d_gate_up[:, column_share:], plans[1]), plans[1])
+    down_total = reduce_scatter(to_payload(d_down, plans[2]), plans[2])
+    qkv_total = reduce_scatter(
+        to_payload(jnp.moveaxis(d_qkv, 0, 1).reshape(features, -1), plans[0]), plans[0]
+    )
+    out_total = reduce_scatter(to_payload(d_out, plans[1]), plans[1])
+    qkv_total = jnp.moveaxis(qkv_total[:rows].reshape(rows, slot_count, -1), 1, 0)
     reduced = (
-        lax.psum_scatter(part_query, "dp", scatter_dimension=1, tiled=True),
-        lax.psum_scatter(part_key, "dp", scatter_dimension=1, tiled=True),
-        lax.psum_scatter(part_value, "dp", scatter_dimension=1, tiled=True),
-        lax.psum_scatter(d_out, "dp", scatter_dimension=2, tiled=True),
-        lax.psum_scatter(part_gate, "dp", scatter_dimension=0, tiled=True),
-        lax.psum_scatter(part_up, "dp", scatter_dimension=0, tiled=True),
-        lax.psum_scatter(d_down, "dp", scatter_dimension=1, tiled=True),
-        lax.psum_scatter(d_attn_gain, "dp", scatter_dimension=0, tiled=True),
-        lax.psum_scatter(d_ffn_gain, "dp", scatter_dimension=0, tiled=True),
+        qkv_total[..., :group_cols],
+        qkv_total[..., group_cols : group_cols + head_size],
+        qkv_total[..., group_cols + head_size :],
+        out_total[:rows].T.reshape(slot_count, group_cols, rows),
+        gate_total[:rows],
+        up_total[:rows],
+        down_total[:rows].T,
+        gate_total[rows, :rows],
+        gate_total[rows, rows : 2 * rows],
     )
     return (
         hidden.astype(jnp.bfloat16)[None],

time: 1250 us -> 811 us (0.65)
  blocking collectives: 450 us -> 0 us
  waiting for transfers between devices: 110 us -> 70.2 us
  local copies, waits for them, and re-layouts: 118 us -> 151 us
  starting transfers between devices: 11.4 us -> 36.8 us
  other arithmetic: 131 us -> 150 us
  matrix products: 390 us -> 372 us
  between operations: 17.2 us -> 2.78 us
    unnamed x2 -> x0, blocking collectives: 450 us -> none
    psum x7 -> x0, waiting for transfers between devices: 103 us -> none  [the longest x2 40.7 us: per_device(): lax.psum(partial_sum.astype(jnp.bfloat16).astype(jnp.float32).astype(jnp....]
    ppermute x0 -> x32, waiting for transfers between devices: none -> 70.2 us  [the longest x24 60.5 us: reduce_stage(): lax.ppermute(outgoing, 'dp', [(i, i ^ mask) for i in range(size)])]
    ppermute x0 -> x32, starting transfers between devices: none -> 36.8 us  [the longest x24 34.4 us: reduce_stage(): lax.ppermute(outgoing, 'dp', [(i, i ^ mask) for i in range(size)])]
    reshape x0 -> x6, local copies, waits for them, and re-layouts: none -> 16.5 us  [the longest x4 14.6 us: to_payload(): shards = grad.astype(jnp.bfloat16).reshape(size, rows, grad.shape[1])]
    convert_element_type x0 -> x3, local copies, waits for them, and re-layouts: none -> 14 us  [to_payload(): shards = grad.astype(jnp.bfloat16).reshape(size, rows, grad.shape[1])]
    dynamic_slice x0 -> x16, local copies, waits for them, and re-layouts: none -> 13 us  [reduce_stage(): lax.dynamic_slice_in_dim(current, (mine ^ offset) * pieces, pieces, 0)]
    unnamed x216 -> x321, local copies, waits for them, and re-layouts: 47.9 us -> 43.9 us
  transfers between devices with their start and end apart: 11 -> 32, of which waited for: 8 -> 12; matrix products, arithmetic and copies ran while one was open for 40% -> 34% of each run, Pallas kernels for 0% -> 0%
where the time goes in v1:
time: 811 us; the launch traced here: 799 us
  matrix products  372 us (46%)
  local copies, waits for them, and re-layouts  151 us (19%)
  other arithmetic  150 us (18%)
  waiting for transfers between devices  70.2 us (9%)
  starting transfers between devices  36.8 us (5%)
  loops' own time  17.2 us (2%)
    sub x8, matrix products, attend_block(): exponent = jnp.exp(scores - row_max)  87.3 us
    ppermute x24, waiting for transfers between devices, reduce_stage(): lax.ppermute(outgoing, 'dp', [(i, i ^ mask) for i in range(size)])  60.5 us
    convert_element_type x4, other arithmetic, backward_one_block(): grad_scores = (probabilities * (grad_probs - delta)).astype(jnp.bfloat16)  50.7 us
    dot_general x4, matrix products, backward_one_block(): jnp.einsum('sqjc,skc->sjqk', grad_block, values_all, preferred_element_ty...  49 us
    unnamed x321, local copies, waits for them, and re-layouts  43.9 us
    dot_general x4, matrix products, backward_one_block(): jnp.einsum('sjqk,sqjc->skc', probabilities.astype(jnp.bfloat16), grad_blo...  36.3 us
    ppermute x24, starting transfers between devices, reduce_stage(): lax.ppermute(outgoing, 'dp', [(i, i ^ mask) for i in range(size)])  34.4 us
    dot_general x4, matrix products, forward_one_block(): jnp.einsum('sjqk,skc->sqjc', probabilities.astype(jnp.bfloat16), forward_...  32.5 us
  transfers between devices with their start and end apart: 32, of which 12 were waited for; matrix products, arithmetic and copies ran while one was open for 34% of the time, Pallas kernels for 0%

profile of v1, /device:TPU:0, one launch (start us, length us, event | category | flops | bytes accessed | tf_op | source)
XLA Modules:
  0.0 799.5 jit_solution(3159250352189884321)
XLA Ops:
  20.3 52.0 %while.54 = (s32[]{:T(128)}, bf16[2,3,512,192]{2,3,1,0:T(8,128)(2,1)}, s32[2]{0:T(128)S(1)}, s32[1024]{0:T(1024)S(1)}, s32[1,1024]{1,0:T(1,128)S(1)}, /*index=5*...) while((s32[]{:T(128)}, ...), condition=%wide.region_5.6_spmd.clone, body=%wide.region_2.5_spmd.clone.sunk | while | flops 1238140416 | bytes 43174568 | solution.py:207
  26.3 10.9 %fusion.383 = (f32[3,3,512]{2,1,0:T(4,128)S(1)}, f32[3,3,512,1024]{3,2,1,0:T(8,128)}) fusion(bf16[3,512,3,64]{1,3,2,0:T(8,128)(2,1)S(1)} %bitcast.542, pred[512,1024]{1,0:T(8,128)(4,1)} %fusion.382, bf16[3,1024,64]{1,2,0:T(8,128)(2,1)S(1)} %get-tuple-element.864), kind=kOutput, calls=%fused_computation.460.clone.1 | convolution fusion | flops 622855168 | bytes 20400128 | tf_op jit(solution)/shard_map/while/body/eval_jaxpr/sub | solution.py:173
  52.2 10.9 %fusion.383 = (f32[3,3,512]{2,1,0:T(4,128)S(1)}, f32[3,3,512,1024]{3,2,1,0:T(8,128)}) fusion(bf16[3,512,3,64]{1,3,2,0:T(8,128)(2,1)S(1)} %bitcast.542, pred[512,1024]{1,0:T(8,128)(4,1)} %fusion.382, bf16[3,1024,64]{1,2,0:T(8,128)(2,1)S(1)} %get-tuple-element.864), kind=kOutput, calls=%fused_computation.460.clone.1 | convolution fusion | flops 622855168 | bytes 20400128 | tf_op jit(solution)/shard_map/while/body/eval_jaxpr/sub | solution.py:173
  114.0 52.0 %while.55 = (s32[]{:T(128)}, bf16[2,3,512,192]{2,3,1,0:T(8,128)(2,1)}, s32[2]{0:T(128)S(1)}, s32[1024]{0:T(1024)S(1)}, s32[1,1024]{1,0:T(1,128)S(1)}, /*index=5*...) while((s32[]{:T(128)}, ...), condition=%wide.region_11.12_spmd.clone, body=%wide.region_8.11_spmd.clone.sunk | while | flops 1238140416 | bytes 43174568 | solution.py:207
  120.1 10.9 %fusion.389 = (f32[3,3,512]{2,1,0:T(4,128)S(1)}, f32[3,3,512,1024]{3,2,1,0:T(8,128)}) fusion(bf16[3,512,3,64]{1,3,2,0:T(8,128)(2,1)S(1)} %bitcast.543, pred[512,1024]{1,0:T(8,128)(4,1)} %fusion.388, bf16[3,1024,64]{1,2,0:T(8,128)(2,1)S(1)} %get-tuple-element.897), kind=kOutput, calls=%fused_computation.461.clone.1 | convolution fusion | flops 622855168 | bytes 20400128 | tf_op jit(solution)/shard_map/while/body/eval_jaxpr/sub | solution.py:173
  146.0 10.9 %fusion.389 = (f32[3,3,512]{2,1,0:T(4,128)S(1)}, f32[3,3,512,1024]{3,2,1,0:T(8,128)}) fusion(bf16[3,512,3,64]{1,3,2,0:T(8,128)(2,1)S(1)} %bitcast.543, pred[512,1024]{1,0:T(8,128)(4,1)} %fusion.388, bf16[3,1024,64]{1,2,0:T(8,128)(2,1)S(1)} %get-tuple-element.897), kind=kOutput, calls=%fused_computation.461.clone.1 | convolution fusion | flops 622855168 | bytes 20400128 | tf_op jit(solution)/shard_map/while/body/eval_jaxpr/sub | solution.py:173
  221.8 133.4 %while.56 = (s32[]{:T(128)}, f32[3,1024,64]{1,2,0:T(8,128)}, f32[3,1024,64]{1,2,0:T(8,128)}, f32[2,3,512,3,64]{2,4,3,1,0:T(8,128)}, s32[2]{0:T(128)S(1)}, /*inde...) while((s32[]{:T(128)}, f32[3,1024,64]{1,2,0:T(8,128)}, ...), condition=%wide.region_18.19_spmd.clone, body=%wide.region_14.18_spmd.clone.sunk | while | flops 3702229504 | bytes 173337328 | solution.py:323
  229.6 10.9 %fusion.404 = (f32[3,3,512]{2,1,0:T(4,128)S(1)}, f32[3,3,512,1024]{3,2,1,0:T(8,128)}) fusion(bf16[3,512,3,64]{1,3,2,0:T(8,128)(2,1)S(1)} %bitcast.528, pred[512,1024]{1,0:T(8,128)(4,1)} %fusion.403, bf16[3,1024,64]{1,2,0:T(8,128)(2,1)S(1)} %get-tuple-element.938), kind=kOutput, calls=%fused_computation.462.clone.1 | convolution fusion | flops 622855168 | bytes 20400128 | tf_op jit(solution)/shard_map/while/body/eval_jaxpr/sub | solution.py:173
  240.5 12.3 %fusion.405 = (f32[3,3,512]{2,1,0:T(4,128)S(1)}, f32[3,512,3,1024]{3,1,2,0:T(8,128)}) fusion(f32[3,3,512,1024]{3,2,1,0:T(8,128)} %get-tuple-element.814, f32[3,3,512]{2,1,0:T(4,128)S(1)} %get-tuple-element.815, bf16[3,512,3,64]{1,3,2,0:T(8,128)(2,1)} %bitcast.538, bf16[3,1024,64]{1,2,0:T(8,128)(2,1)} %get-tuple-element.940), kind=kOutput, calls=%fused_computation.55.clone.1 | convolution fusion | flops 618130944 | bytes 38768640 | tf_op jit(solution)/shard_map/while/body/eval_jaxpr/sqjc,skc->sjqk/dot_general | solution.py:293
  252.7 12.7 %fusion.406 = bf16[3,3,512,1024]{3,2,1,0:T(8,128)(2,1)S(1)} fusion(f32[3,512,3,1024]{3,1,2,0:T(8,128)} %get-tuple-element.817, f32[3,3,512]{2,1,0:T(4,128)S(1)} %get-tuple-element.818, f32[3,3,512,1024]{3,2,1,0:T(8,128)} %get-tuple-element.814, f32[3,3,512]{2,1,0:T(4,128)S(1)} %get-tuple-element.815), kind=kLoop, calls=%fused_computation.57.clone.1 | loop fusion | flops 18874368 | bytes 47222784 | tf_op jit(solution)/shard_map/while/body/eval_jaxpr/convert_element_type | solution.py:297
  295.7 10.9 %fusion.404 = (f32[3,3,512]{2,1,0:T(4,128)S(1)}, f32[3,3,512,1024]{3,2,1,0:T(8,128)}) fusion(bf16[3,512,3,64]{1,3,2,0:T(8,128)(2,1)S(1)} %bitcast.528, pred[512,1024]{1,0:T(8,128)(4,1)} %fusion.403, bf16[3,1024,64]{1,2,0:T(8,128)(2,1)S(1)} %get-tuple-element.938), kind=kOutput, calls=%fused_computation.462.clone.1 | convolution fusion | flops 622855168 | bytes 20400128 | tf_op jit(solution)/shard_map/while/body/eval_jaxpr/sub | solution.py:173
  306.6 12.3 %fusion.405 = (f32[3,3,512]{2,1,0:T(4,128)S(1)}, f32[3,512,3,1024]{3,1,2,0:T(8,128)}) fusion(f32[3,3,512,1024]{3,2,1,0:T(8,128)} %get-tuple-element.814, f32[3,3,512]{2,1,0:T(4,128)S(1)} %get-tuple-element.815, bf16[3,512,3,64]{1,3,2,0:T(8,128)(2,1)} %bitcast.538, bf16[3,1024,64]{1,2,0:T(8,128)(2,1)} %get-tuple-element.940), kind=kOutput, calls=%fused_computation.55.clone.1 | convolution fusion | flops 618130944 | bytes 38768640 | tf_op jit(solution)/shard_map/while/body/eval_jaxpr/sqjc,skc->sjqk/dot_general | solution.py:293
  318.9 12.7 %fusion.406 = bf16[3,3,512,1024]{3,2,1,0:T(8,128)(2,1)S(1)} fusion(f32[3,512,3,1024]{3,1,2,0:T(8,128)} %get-tuple-element.817, f32[3,3,512]{2,1,0:T(4,128)S(1)} %get-tuple-element.818, f32[3,3,512,1024]{3,2,1,0:T(8,128)} %get-tuple-element.814, f32[3,3,512]{2,1,0:T(4,128)S(1)} %get-tuple-element.815), kind=kLoop, calls=%fused_computation.57.clone.1 | loop fusion | flops 18874368 | bytes 47222784 | tf_op jit(solution)/shard_map/while/body/eval_jaxpr/convert_element_type | solution.py:297
  387.3 10.8 %multiply_convert_fusion.1 = (bf16[1024,1280]{1,0:T(8,128)(2,1)}, bf16[1024,1280]{1,0:T(8,128)(2,1)}) fusion(f32[1024,2560]{1,0:T(8,128)} %copy-done.38, bf16[1280,960]{0,1:T(8,128)(2,1)S(1)} %copy-done, f32[1024,960]{0,1:T(8,128)S(1)} %subtract_add_fusion.1), kind=kOutput, calls=%fused_computation.161 | convolution fusion | flops 2534604800 | bytes 22118400 | tf_op jit(solution)/shard_map/ld,fd->lf/dot_general | solution.py:262
  406.2 11.8 %add_convert_fusion = bf16[960,2560]{1,0:T(8,128)(2,1)S(1)} fusion(f32[960,2560]{1,0:T(8,128)} %fusion.184, bf16[1024,1280]{1,0:T(8,128)(2,1)} %get-tuple-element.517, bf16[1024,1280]{1,0:T(8,128)(2,1)} %get-tuple-element.516, f32[1024,960]{0,1:T(8,128)} %copy-done.11, f32[960]{0:T(1024)S(1)} %copy-done.92, f32[1024]{0:T(1024)S(1)} %copy-done.97), kind=kOutput, calls=%fused_computation.145 | convolution fusion | flops 5051514880 | bytes 23928576 | tf_op jit(solution)/shard_map/ld,lf->df/dot_general | solution.py:272
  448.5 11.9 %collective-permute-done.28 = bf16[8,64,1280]{2,1,0:T(8,128)(2,1)} collective-permute-done((bf16[8,64,1280]{2,1,0:T(8,128)(2,1)}, bf16[8,64,1280]{2,1,0:T(8,128)(2,1)}, u32[]{:S(2)}, u32[]{:S(2)}) %collective-permute-start.28) | collective-permute-done | bytes 1310752 | tf_op jit(solution)/shard_map/ppermute | solution.py:90
  482.3 133.4 %while.57 = (s32[]{:T(128)}, f32[3,1024,64]{1,2,0:T(8,128)}, f32[3,1024,64]{1,2,0:T(8,128)}, f32[2,3,512,3,64]{2,4,3,1,0:T(8,128)}, s32[2]{0:T(128)S(1)}, /*inde...) while((s32[]{:T(128)}, f32[3,1024,64]{1,2,0:T(8,128)}, ...), condition=%wide.region_25.26_spmd.clone, body=%wide.region_21.25_spmd.clone.sunk | while | flops 3702229504 | bytes 173337328 | solution.py:323
  489.8 10.9 %fusion.423 = (f32[3,3,512]{2,1,0:T(4,128)S(1)}, f32[3,3,512,1024]{3,2,1,0:T(8,128)}) fusion(bf16[3,512,3,64]{1,3,2,0:T(8,128)(2,1)S(1)} %bitcast.531, pred[512,1024]{1,0:T(8,128)(4,1)} %fusion.422, bf16[3,1024,64]{1,2,0:T(8,128)(2,1)S(1)} %get-tuple-element.980), kind=kOutput, calls=%fused_computation.463.clone.1 | convolution fusion | flops 622855168 | bytes 20400128 | tf_op jit(solution)/shard_map/while/body/eval_jaxpr/sub | solution.py:173
  500.7 12.3 %fusion.424 = (f32[3,3,512]{2,1,0:T(4,128)S(1)}, f32[3,512,3,1024]{3,1,2,0:T(8,128)}) fusion(f32[3,3,512,1024]{3,2,1,0:T(8,128)} %get-tuple-element.831, f32[3,3,512]{2,1,0:T(4,128)S(1)} %get-tuple-element.832, bf16[3,512,3,64]{1,3,2,0:T(8,128)(2,1)} %bitcast.540, bf16[3,1024,64]{1,2,0:T(8,128)(2,1)} %get-tuple-element.982), kind=kOutput, calls=%fused_computation.94.clone.1 | convolution fusion | flops 618130944 | bytes 38768640 | tf_op jit(solution)/shard_map/while/body/eval_jaxpr/sqjc,skc->sjqk/dot_general | solution.py:293
  513.0 12.7 %fusion.425 = bf16[3,3,512,1024]{3,2,1,0:T(8,128)(2,1)S(1)} fusion(f32[3,512,3,1024]{3,1,2,0:T(8,128)} %get-tuple-element.834, f32[3,3,512]{2,1,0:T(4,128)S(1)} %get-tuple-element.835, f32[3,3,512,1024]{3,2,1,0:T(8,128)} %get-tuple-element.831, f32[3,3,512]{2,1,0:T(4,128)S(1)} %get-tuple-element.832), kind=kLoop, calls=%fused_computation.96.clone.1 | loop fusion | flops 18874368 | bytes 47222784 | tf_op jit(solution)/shard_map/while/body/eval_jaxpr/convert_element_type | solution.py:297
  555.9 10.9 %fusion.423 = (f32[3,3,512]{2,1,0:T(4,128)S(1)}, f32[3,3,512,1024]{3,2,1,0:T(8,128)}) fusion(bf16[3,512,3,64]{1,3,2,0:T(8,128)(2,1)S(1)} %bitcast.531, pred[512,1024]{1,0:T(8,128)(4,1)} %fusion.422, bf16[3,1024,64]{1,2,0:T(8,128)(2,1)S(1)} %get-tuple-element.980), kind=kOutput, calls=%fused_computation.463.clone.1 | convolution fusion | flops 622855168 | bytes 20400128 | tf_op jit(solution)/shard_map/while/body/eval_jaxpr/sub | solution.py:173
  566.8 12.3 %fusion.424 = (f32[3,3,512]{2,1,0:T(4,128)S(1)}, f32[3,512,3,1024]{3,1,2,0:T(8,128)}) fusion(f32[3,3,512,1024]{3,2,1,0:T(8,128)} %get-tuple-element.831, f32[3,3,512]{2,1,0:T(4,128)S(1)} %get-tuple-element.832, bf16[3,512,3,64]{1,3,2,0:T(8,128)(2,1)} %bitcast.540, bf16[3,1024,64]{1,2,0:T(8,128)(2,1)} %get-tuple-element.982), kind=kOutput, calls=%fused_computation.94.clone.1 | convolution fusion | flops 618130944 | bytes 38768640 | tf_op jit(solution)/shard_map/while/body/eval_jaxpr/sqjc,skc->sjqk/dot_general | solution.py:293
  579.1 12.7 %fusion.425 = bf16[3,3,512,1024]{3,2,1,0:T(8,128)(2,1)S(1)} fusion(f32[3,512,3,1024]{3,1,2,0:T(8,128)} %get-tuple-element.834, f32[3,3,512]{2,1,0:T(4,128)S(1)} %get-tuple-element.835, f32[3,3,512,1024]{3,2,1,0:T(8,128)} %get-tuple-element.831, f32[3,3,512]{2,1,0:T(4,128)S(1)} %get-tuple-element.832), kind=kLoop, calls=%fused_computation.96.clone.1 | loop fusion | flops 18874368 | bytes 47222784 | tf_op jit(solution)/shard_map/while/body/eval_jaxpr/convert_element_type | solution.py:297
  705.4 11.3 %collective-permute-done.14 = bf16[4,64,576]{2,1,0:T(8,128)(2,1)S(1)} collective-permute-done((bf16[4,64,576]{2,1,0:T(8,128)(2,1)S(1)}, bf16[4,64,576]{2,1,0:T(8,128)(2,1)S(1)}, u32[]{:S(2)}, u32[]{:S(2)}) %collective-permute-start.14) | collective-permute-done | bytes 294944 | tf_op jit(solution)/shard_map/ppermute | solution.py:90
  (618 shorter events, 546.7 us)
Async XLA Ops:
  365.4 13.9 %collective-permute-start.5 = (bf16[1024,960]{0,1:T(8,128)(2,1)}, bf16[1024,960]{0,1:T(8,128)(2,1)}, u32[]{:S(2)}, u32[]{:S(2)}) collective-permute-start(bf16[1024,960]{0,1:T(8,128)(2,1)} %bitcast_convert_fusion.1), channel_id=1, source_target_pairs={{0,1},{1,0},{2,3},{3,2},{4,5},{5,4},{6,7},{7,6},{8,9},{9,8},{10,11... | collective-permute-start | bytes 5898248 | tf_op jit(solution)/shard_map/ppermute | solution.py:46
  428.1 32.4 %collective-permute-start.28 = (bf16[8,64,1280]{2,1,0:T(8,128)(2,1)}, bf16[8,64,1280]{2,1,0:T(8,128)(2,1)}, u32[]{:S(2)}, u32[]{:S(2)}) collective-permute-start(bf16[8,64,1280]{2,1,0:T(8,128)(2,1)} %constant_dynamic-slice_fusion.9), channel_id=1, source_target_pairs={{0,8},{2,10},{4,12},{6,14},{8,0},{10,2},{12,4},{14,6},{16,24},{18,... | collective-permute-start | bytes 3932168 | tf_op jit(solution)/shard_map/ppermute | solution.py:90
  433.9 31.5 %collective-permute-start.23 = (bf16[8,64,1280]{2,1,0:T(8,128)(2,1)}, bf16[8,64,1280]{2,1,0:T(8,128)(2,1)}, u32[]{:S(2)}, u32[]{:S(2)}) collective-permute-start(bf16[8,64,1280]{2,1,0:T(8,128)(2,1)} %constant_dynamic-slice_fusion.14), channel_id=1, source_target_pairs={{0,4},{2,6},{4,0},{6,2},{8,12},{10,14},{12,8},{14,10},{16,20},{18,... | collective-permute-start | bytes 3932168 | tf_op jit(solution)/shard_map/ppermute | solution.py:90
  443.0 27.1 %collective-permute-start.6 = (bf16[1024,960]{0,1:T(8,128)(2,1)}, bf16[1024,960]{0,1:T(8,128)(2,1)}, u32[]{:S(2)}, u32[]{:S(2)}) collective-permute-start(bf16[1024,960]{0,1:T(8,128)(2,1)} %fusion.200), channel_id=1, source_target_pairs={{0,1},{1,0},{2,3},{3,2},{4,5},{5,4},{6,7},{7,6},{8,9},{9,8},{10,11... | collective-permute-start | bytes 5898248 | tf_op jit(solution)/shard_map/ppermute | solution.py:46
  463.5 215.0 %collective-permute-start.29 = (bf16[4,64,1280]{2,1,0:T(8,128)(2,1)}, bf16[4,64,1280]{2,1,0:T(8,128)(2,1)}, u32[]{:S(2)}, u32[]{:S(2)}) collective-permute-start(bf16[4,64,1280]{2,1,0:T(8,128)(2,1)} %constant_dynamic-slice_fusion.8), channel_id=1, source_target_pairs={{0,2},{2,0},{4,6},{6,4},{8,10},{10,8},{12,14},{14,12},{16,18},{18,... | collective-permute-start | bytes 1966088 | tf_op jit(solution)/shard_map/ppermute | solution.py:90
  468.4 161.1 %collective-permute-start.24 = (bf16[4,64,1280]{2,1,0:T(8,128)(2,1)}, bf16[4,64,1280]{2,1,0:T(8,128)(2,1)}, u32[]{:S(2)}, u32[]{:S(2)}) collective-permute-start(bf16[4,64,1280]{2,1,0:T(8,128)(2,1)} %constant_dynamic-slice_fusion.13), channel_id=1, source_target_pairs={{0,2},{2,0},{4,6},{6,4},{8,10},{10,8},{12,14},{14,12},{16,18},{18,... | collective-permute-start | bytes 1966088 | tf_op jit(solution)/shard_map/ppermute | solution.py:90
  631.6 52.3 %collective-permute-start.25 = (bf16[1,64,1280]{2,1,0:T(8,128)(2,1)}, bf16[1,64,1280]{2,1,0:T(8,128)(2,1)}, u32[]{:S(2)}, u32[]{:S(2)}) collective-permute-start(bf16[1,64,1280]{2,1,0:T(8,128)(2,1)} %get-tuple-element.541), channel_id=1, source_target_pairs={{0,16},{2,18},{4,20},{6,22},{8,24},{10,26},{12,28},{14,30},{16,0},... | collective-permute-start | bytes 491528 | tf_op jit(solution)/shard_map/ppermute | solution.py:90
  634.3 50.2 %collective-permute-start.26 = (bf16[1,64,1280]{2,1,0:T(8,128)(2,1)}, bf16[1,64,1280]{2,1,0:T(8,128)(2,1)}, u32[]{:S(2)}, u32[]{:S(2)}) collective-permute-start(bf16[1,64,1280]{2,1,0:T(8,128)(2,1)} %get-tuple-element.543), channel_id=1, source_target_pairs={{0,8},{2,10},{4,12},{6,14},{8,0},{10,2},{12,4},{14,6},{16,24},{18,... | collective-permute-start | bytes 491528 | tf_op jit(solution)/shard_map/ppermute | solution.py:90
  635.8 49.3 %collective-permute-start.27 = (bf16[1,64,1280]{2,1,0:T(8,128)(2,1)}, bf16[1,64,1280]{2,1,0:T(8,128)(2,1)}, u32[]{:S(2)}, u32[]{:S(2)}) collective-permute-start(bf16[1,64,1280]{2,1,0:T(8,128)(2,1)} %get-tuple-element.542), channel_id=1, source_target_pairs={{0,24},{2,26},{4,28},{6,30},{8,16},{10,18},{12,20},{14,22},{16,8},... | collective-permute-start | bytes 491528 | tf_op jit(solution)/shard_map/ppermute | solution.py:90
  636.0 86.5 %collective-permute-start.7 = (bf16[1024,960]{0,1:T(8,128)(2,1)}, bf16[1024,960]{0,1:T(8,128)(2,1)}, u32[]{:S(2)}, u32[]{:S(2)}) collective-permute-start(bf16[1024,960]{0,1:T(8,128)(2,1)} %bitcast_convert_fusion), channel_id=1, source_target_pairs={{0,1},{1,0},{2,3},{3,2},{4,5},{5,4},{6,7},{7,6},{8,9},{9,8},{10,11... | collective-permute-start | bytes 5898248 | tf_op jit(solution)/shard_map/ppermute | solution.py:46
  678.5 17.8 %collective-permute-start.13 = (bf16[8,64,576]{2,1,0:T(8,128)(2,1)}, bf16[8,64,576]{2,1,0:T(8,128)(2,1)}, u32[]{:S(2)}, u32[]{:S(2)}) collective-permute-start(bf16[8,64,576]{2,1,0:T(8,128)(2,1)} %constant_dynamic-slice_fusion.24), channel_id=1, source_target_pairs={{0,4},{2,6},{4,0},{6,2},{8,12},{10,14},{12,8},{14,10},{16,20},{18,... | collective-permute-start | bytes 1769480 | tf_op jit(solution)/shard_map/ppermute | solution.py:90
  684.0 18.9 %collective-permute-start.30 = (bf16[2,64,1280]{2,1,0:T(8,128)(2,1)S(1)}, bf16[2,64,1280]{2,1,0:T(8,128)(2,1)S(1)}, u32[]{:S(2)}, u32[]{:S(2)}) collective-permute-start(bf16[2,64,1280]{2,1,0:T(8,128)(2,1)S(1)} %constant_dynamic-slice_fusion.7), channel_id=1, source_target_pairs={{0,4},{2,6},{4,0},{6,2},{8,12},{10,14},{12,8},{14,10},{16,20},{18,... | collective-permute-start | bytes 983048 | tf_op jit(solution)/shard_map/ppermute | solution.py:90
  684.5 51.3 %collective-permute-start.8 = (bf16[8,64,960]{2,1,0:T(8,128)(2,1)}, bf16[8,64,960]{2,1,0:T(8,128)(2,1)}, u32[]{:S(2)}, u32[]{:S(2)}) collective-permute-start(bf16[8,64,960]{2,1,0:T(8,128)(2,1)} %constant_dynamic-slice_fusion.29), channel_id=1, source_target_pairs={{0,2},{2,0},{4,6},{6,4},{8,10},{10,8},{12,14},{14,12},{16,18},{18,... | collective-permute-start | bytes 2949128 | tf_op jit(solution)/shard_map/ppermute | solution.py:90
  697.8 18.9 %collective-permute-start.14 = (bf16[4,64,576]{2,1,0:T(8,128)(2,1)S(1)}, bf16[4,64,576]{2,1,0:T(8,128)(2,1)S(1)}, u32[]{:S(2)}, u32[]{:S(2)}) collective-permute-start(bf16[4,64,576]{2,1,0:T(8,128)(2,1)S(1)} %constant_dynamic-slice_fusion.23), channel_id=1, source_target_pairs={{0,2},{2,0},{4,6},{6,4},{8,10},{10,8},{12,14},{14,12},{16,18},{18,... | collective-permute-start | bytes 884744 | tf_op jit(solution)/shard_map/ppermute | solution.py:90
  703.7 36.5 %collective-permute-start.31 = (bf16[1,64,1280]{2,1,0:T(8,128)(2,1)}, bf16[1,64,1280]{2,1,0:T(8,128)(2,1)}, u32[]{:S(2)}, u32[]{:S(2)}) collective-permute-start(bf16[1,64,1280]{2,1,0:T(8,128)(2,1)} %constant_dynamic-slice_fusion.6), channel_id=1, source_target_pairs={{0,16},{2,18},{4,20},{6,22},{8,24},{10,26},{12,28},{14,30},{16,0},... | collective-permute-start | bytes 491528 | tf_op jit(solution)/shard_map/ppermute | solution.py:90
  718.3 25.1 %collective-permute-start.15 = (bf16[1,64,576]{2,1,0:T(8,128)(2,1)}, bf16[1,64,576]{2,1,0:T(8,128)(2,1)}, u32[]{:S(2)}, u32[]{:S(2)}) collective-permute-start(bf16[1,64,576]{2,1,0:T(8,128)(2,1)} %get-tuple-element.554), channel_id=1, source_target_pairs={{0,16},{2,18},{4,20},{6,22},{8,24},{10,26},{12,28},{14,30},{16,0},... | collective-permute-start | bytes 221192 | tf_op jit(solution)/shard_map/ppermute | solution.py:90
  720.0 23.4 %collective-permute-start.16 = (bf16[1,64,576]{2,1,0:T(8,128)(2,1)}, bf16[1,64,576]{2,1,0:T(8,128)(2,1)}, u32[]{:S(2)}, u32[]{:S(2)}) collective-permute-start(bf16[1,64,576]{2,1,0:T(8,128)(2,1)} %get-tuple-element.556), channel_id=1, source_target_pairs={{0,8},{2,10},{4,12},{6,14},{8,0},{10,2},{12,4},{14,6},{16,24},{18,... | collective-permute-start | bytes 221192 | tf_op jit(solution)/shard_map/ppermute | solution.py:90
  722.5 20.9 %collective-permute-start.17 = (bf16[1,64,576]{2,1,0:T(8,128)(2,1)}, bf16[1,64,576]{2,1,0:T(8,128)(2,1)}, u32[]{:S(2)}, u32[]{:S(2)}) collective-permute-start(bf16[1,64,576]{2,1,0:T(8,128)(2,1)} %get-tuple-element.555), channel_id=1, source_target_pairs={{0,24},{2,26},{4,28},{6,30},{8,16},{10,18},{12,20},{14,22},{16,8},... | collective-permute-start | bytes 221192 | tf_op jit(solution)/shard_map/ppermute | solution.py:90
  736.7 29.3 %collective-permute-start.18 = (bf16[8,64,1280]{2,1,0:T(8,128)(2,1)}, bf16[8,64,1280]{2,1,0:T(8,128)(2,1)}, u32[]{:S(2)}, u32[]{:S(2)}) collective-permute-start(bf16[8,64,1280]{2,1,0:T(8,128)(2,1)} %constant_dynamic-slice_fusion.19), channel_id=1, source_target_pairs={{0,2},{2,0},{4,6},{6,4},{8,10},{10,8},{12,14},{14,12},{16,18},{18,... | collective-permute-start | bytes 3932168 | tf_op jit(solution)/shard_map/ppermute | solution.py:90
  740.2 12.5 %collective-permute-start.9 = (bf16[4,64,960]{2,1,0:T(8,128)(2,1)}, bf16[4,64,960]{2,1,0:T(8,128)(2,1)}, u32[]{:S(2)}, u32[]{:S(2)}) collective-permute-start(bf16[4,64,960]{2,1,0:T(8,128)(2,1)} %constant_dynamic-slice_fusion.28), channel_id=1, source_target_pairs={{0,4},{2,6},{4,0},{6,2},{8,12},{10,14},{12,8},{14,10},{16,20},{18,... | collective-permute-start | bytes 1474568 | tf_op jit(solution)/shard_map/ppermute | solution.py:90
  754.0 17.2 %collective-permute-start.10 = (bf16[1,64,960]{2,1,0:T(8,128)(2,1)S(1)}, bf16[1,64,960]{2,1,0:T(8,128)(2,1)S(1)}, u32[]{:S(2)}, u32[]{:S(2)}) collective-permute-start(bf16[1,64,960]{2,1,0:T(8,128)(2,1)S(1)} %get-tuple-element.547), channel_id=1, source_target_pairs={{0,16},{2,18},{4,20},{6,22},{8,24},{10,26},{12,28},{14,30},{16,0},... | collective-permute-start | bytes 368648 | tf_op jit(solution)/shard_map/ppermute | solution.py:90
  755.6 15.7 %collective-permute-start.11 = (bf16[1,64,960]{2,1,0:T(8,128)(2,1)S(1)}, bf16[1,64,960]{2,1,0:T(8,128)(2,1)S(1)}, u32[]{:S(2)}, u32[]{:S(2)}) collective-permute-start(bf16[1,64,960]{2,1,0:T(8,128)(2,1)S(1)} %get-tuple-element.549), channel_id=1, source_target_pairs={{0,8},{2,10},{4,12},{6,14},{8,0},{10,2},{12,4},{14,6},{16,24},{18,... | collective-permute-start | bytes 368648 | tf_op jit(solution)/shard_map/ppermute | solution.py:90
  758.1 13.1 %collective-permute-start.12 = (bf16[1,64,960]{2,1,0:T(8,128)(2,1)S(1)}, bf16[1,64,960]{2,1,0:T(8,128)(2,1)S(1)}, u32[]{:S(2)}, u32[]{:S(2)}) collective-permute-start(bf16[1,64,960]{2,1,0:T(8,128)(2,1)S(1)} %get-tuple-element.548), channel_id=1, source_target_pairs={{0,24},{2,26},{4,28},{6,30},{8,16},{10,18},{12,20},{14,22},{16,8},... | collective-permute-start | bytes 368648 | tf_op jit(solution)/shard_map/ppermute | solution.py:90
  769.7 14.4 %collective-permute-start.19 = (bf16[4,64,1280]{2,1,0:T(8,128)(2,1)}, bf16[4,64,1280]{2,1,0:T(8,128)(2,1)}, u32[]{:S(2)}, u32[]{:S(2)}) collective-permute-start(bf16[4,64,1280]{2,1,0:T(8,128)(2,1)} %constant_dynamic-slice_fusion.18), channel_id=1, source_target_pairs={{0,4},{2,6},{4,0},{6,2},{8,12},{10,14},{12,8},{14,10},{16,20},{18,... | collective-permute-start | bytes 1966088 | tf_op jit(solution)/shard_map/ppermute | solution.py:90
  (139 other events, 912.6 us)

commit v2 on v1

v2 whole, which is shorter than its diff:
```python
import functools
import math

import jax
import jax.numpy as jnp
import numpy as np
from jax import lax
from jax.experimental import pallas as pl
from jax.experimental.pallas import tpu as pltpu
from jax.sharding import PartitionSpec as P

REPEAT = 2
BLOCK = 256
FFN_BLOCK = 256
LANES = 128
HEAD = 64
VROWS = 80
epsilon = 1e-05
masked_value = -1e30
LOG2E = math.log2(math.e)
LN2 = math.log(2.0)
f32 = jnp.float32
bf16 = jnp.bfloat16
NN = (((1,), (0,)), ((), ()))
NT = (((1,), (1,)), ((), ()))
TN = (((0,), (0,)), ((), ()))
MIB = 1024 * 1024


def matmul(a, b, dims=NN):
    return lax.dot_general(a, b, dims, preferred_element_type=f32)


def wide(column, width):
    return jnp.concatenate([column] * (width // LANES), axis=1)


def inverse_rms(values):
    return lax.rsqrt(jnp.mean(values * values, axis=0, keepdims=True) + epsilon)


def normalise(values, gain):
    return (values * inverse_rms(values) * wide(gain, values.shape[1])).astype(bf16)


def norm_back(values, gain, grad_normed):
    inverse = inverse_rms(values)
    scaled = grad_normed * wide(gain, values.shape[1])
    inner_mean = jnp.mean(scaled * values, axis=0, keepdims=True)
    return inverse * scaled - values * (inverse * inverse * inverse * inner_mean)


def joined_sum(own_ref, other_ref):
    return own_ref[...].astype(f32) + other_ref[...].astype(f32)


def three_parts(value):
    high = value.astype(bf16).astype(f32)
    rest = value - high
    middle = rest.astype(bf16).astype(f32)
    return high, middle, rest - middle


def part_rows(value, first):
    row = lax.broadcasted_iota(jnp.int32, (8, value.shape[1]), 0)
    out = jnp.zeros((8, value.shape[1]), f32)
    for number, part in enumerate(three_parts(value)):
        out = jnp.where(row == first + number, part, out)
    return out


def causal_bias():
    key = lax.broadcasted_iota(jnp.int32, (BLOCK, BLOCK), 0)
    query = lax.broadcasted_iota(jnp.int32, (BLOCK, BLOCK), 1)
    return jnp.where(key <= query, 0.0, masked_value)


def reaches(segments, step, back):
    last = jnp.maximum((step - back + 1) * BLOCK - 1, 0)
    return (step >= back) & (segments[last] == segments[step * BLOCK])


def block_at(index):
    return pl.ds(pl.multiple_of(index * BLOCK, BLOCK), BLOCK)


def turn(upper, lower, cosine, sine):
    return upper * cosine - lower * sine, lower * cosine + upper * sine


def attention_forward(joined, slots, heads, segments, *refs):
    refs = list(refs)
    hidden = refs.pop(0)[...].astype(f32)
    if joined:
        hidden = hidden + joined_sum(refs.pop(0), refs.pop(0))
    gain_ref, wqkv_ref, wout_ref, cos_ref, sin_ref, segment_ref = refs[:6]
    refs = refs[6:]
    if joined:
        refs.pop(0)[...] = hidden
    (normed_out, query_out, key_out, turned_key_out, value_out, attended_out, partial_out,
     turned_value, tri_ref) = refs
    step = pl.program_id(0)
    here = block_at(step)

    @pl.when(step == 0)
    def _():
        tri_ref[...] = causal_bias()

    normed = normalise(hidden, gain_ref[...])
    normed_out[...] = normed
    projected = matmul(wqkv_ref[...], normed)
    cosine, sine = cos_ref[...], sin_ref[...]
    total = slots * heads
    half = HEAD // 2

    same = lax.broadcasted_iota(jnp.int32, (8, BLOCK), 0) == segment_ref[...]
    query_rows = jnp.where(same, 1.0, 0.0)
    key_rows = jnp.where(same, 0.0, masked_value)
    row = lax.broadcasted_iota(jnp.int32, (8, BLOCK), 0)
    minus_rows = jnp.where(row < 3, -1.0, 0.0)
    scale = LOG2E / math.sqrt(HEAD)

    def rows_of(head):
        return projected[head * HEAD : (head + 1) * HEAD]

    for h in range(total + slots):
        piece = rows_of(h)
        upper, lower = turn(piece[:half], piece[half:], cosine, sine)
        if h < total:
            base = h * LANES
            query_out[base : base + HEAD, :] = jnp.concatenate(
                [upper * scale, lower * scale], axis=0
            ).astype(bf16)
            query_out[base + HEAD : base + LANES, :] = jnp.concatenate(
                [query_rows, jnp.zeros((LANES - HEAD - 8, BLOCK), f32)], axis=0
            ).astype(bf16)
        else:
            s = h - total
            turned_key_out[s * HEAD : (s + 1) * HEAD, :] = jnp.concatenate(
                [upper, lower], axis=0
            ).astype(bf16)
            whole = jnp.concatenate(
                [upper, lower, key_rows, minus_rows, jnp.zeros((LANES - HEAD - 16, BLOCK), f32)],
                axis=0,
            )
            key_out[here, s * LANES : (s + 1) * LANES] = whole.T.astype(bf16)
    for s in range(slots):
        value = rows_of(total + slots + s)
        value = jnp.concatenate([value, jnp.ones((LANES - HEAD, BLOCK), f32)], axis=0)
        value_out[here, s * LANES : (s + 1) * LANES] = value.T.astype(bf16)
        turned_value[s * VROWS : (s + 1) * VROWS, here] = value[:VROWS].astype(bf16)

    def attend(blocks):
        width = blocks * BLOCK
        keys = pl.ds(pl.multiple_of((step + 1 - blocks) * BLOCK, BLOCK), width)
        for s in range(slots):
            key = key_out[keys, s * LANES : (s + 1) * LANES]
            value = turned_value[s * VROWS : (s + 1) * VROWS, keys]
            for j in range(heads):
                h = s * heads + j
                scores = matmul(key, query_out[h * LANES : (h + 1) * LANES, :])
                last = scores[width - BLOCK :] + tri_ref[...]
                if blocks > 1:
                    scores = jnp.concatenate([scores[: width - BLOCK], last], axis=0)
                else:
                    scores = last
                top = jnp.max(scores, axis=0, keepdims=True)
                weights = jnp.exp2(scores - top).astype(bf16)
                summed = matmul(value, weights)
                weight_sum = summed[HEAD : HEAD + 1]
                attended_out[h * HEAD : (h + 1) * HEAD, :] = (
                    summed[:HEAD] * (1.0 / weight_sum)
                ).astype(bf16)
                query_out[h * LANES + HEAD : h * LANES + HEAD + 16, :] = jnp.concatenate(
                    [query_rows, part_rows(top + jnp.log2(weight_sum), 0)], axis=0
                ).astype(bf16)

    one = reaches(segments, step, 1)
    two = reaches(segments, step, 2)
    pl.when(jnp.logical_not(one))(functools.partial(attend, 1))
    pl.when(one & jnp.logical_not(two))(functools.partial(attend, 2))
    pl.when(two)(functools.partial(attend, 3))
    partial_out[...] = matmul(wout_ref[...], attended_out[...], TN).astype(bf16)


def token_spec(rows, width=BLOCK):
    return pl.BlockSpec((rows, width), lambda i, *_: (0, i))


def full_spec(shape):
    return pl.BlockSpec(
        shape, lambda *_: (0,) * len(shape), pipeline_mode=pl.Buffered(buffer_count=1)
    )


def out_full_spec(shape):
    return pl.BlockSpec(shape, lambda *_: (0,) * len(shape))


shape_of = jax.ShapeDtypeStruct


def call_attention_forward(segments, parts, gain, wqkv, wout, cosine, sine, slots, heads):
    features, length = parts[0].shape
    joined = len(parts) == 3
    total = slots * heads
    big = shape_of((features, length), bf16)
    outs = [
        (big, token_spec(features)),
        (shape_of((total * LANES, length), bf16), token_spec(total * LANES)),
        (shape_of((length, slots * LANES), bf16), out_full_spec((length, slots * LANES))),
        (shape_of((slots * HEAD, length), bf16), token_spec(slots * HEAD)),
        (shape_of((length, slots * LANES), bf16), out_full_spec((length, slots * LANES))),
        (shape_of((total * HEAD, length), bf16), token_spec(total * HEAD)),
        (big, token_spec(features)),
    ]
    if joined:
        outs.insert(0, (shape_of((features, length), f32), token_spec(features)))
    return pl.pallas_call(
        functools.partial(attention_forward, joined, slots, heads),
        grid_spec=pltpu.PrefetchScalarGridSpec(
            num_scalar_prefetch=1,
            grid=(length // BLOCK,),
            in_specs=[token_spec(features)] * len(parts)
            + [full_spec(a.shape) for a in (gain, wqkv, wout)]
            + [token_spec(HEAD // 2)] * 2
            + [token_spec(1)],
            out_specs=[spec for _, spec in outs],
            scratch_shapes=[
                pltpu.VMEM((slots * VROWS, length), bf16),
                pltpu.VMEM((BLOCK, BLOCK), f32),
            ],
        ),
        out_shape=[shape for shape, _ in outs],
        compiler_params=pltpu.CompilerParams(vmem_limit_bytes=32 * MIB),
        name="attention_forward",
    )(segments, *parts, gain, wqkv, wout, cosine, sine, segments[None, :])


def ffn_forward(hidden_ref, own_ref, other_ref, gain_ref, gate_ref, up_ref, down_ref,
                middle_out, normed_out, gate_out, lift_out, inner_out, partial_out):
    middle = hidden_ref[...].astype(f32) + joined_sum(own_ref, other_ref)
    middle_out[...] = middle
    normed = normalise(middle, gain_ref[...])
    normed_out[...] = normed
    gate = matmul(gate_ref[...], normed, TN)
    lift = matmul(up_ref[...], normed, TN)
    gate_out[...] = gate.astype(bf16)
    lift_out[...] = lift.astype(bf16)
    inner = (gate * jax.nn.sigmoid(gate) * lift).astype(bf16)
    inner_out[...] = inner
    partial_out[...] = matmul(down_ref[...], inner).astype(bf16)


def call_ffn_forward(hidden, own, other, gain, w_gate, w_up, w_down):
    features, length = hidden.shape
    units = w_gate.shape[1]
    spec = functools.partial(token_spec, width=FFN_BLOCK)
    return pl.pallas_call(
        ffn_forward,
        grid=(length // FFN_BLOCK,),
        in_specs=[spec(features)] * 3 + [full_spec(a.shape) for a in (gain, w_gate, w_up, w_down)],
        out_specs=[spec(features)] * 2 + [spec(units)] * 3 + [spec(features)],
        out_shape=[shape_of((features, length), f32), shape_of((features, length), bf16)]
        + [shape_of((units, length), bf16)] * 3
        + [shape_of((features, length), bf16)],
        compiler_params=pltpu.CompilerParams(vmem_limit_bytes=40 * MIB),
        name="ffn_forward",
    )(hidden, own, other, gain, w_gate, w_up, w_down)


def ffn_backward(joined, *refs):
    refs = list(refs)
    grad = refs.pop(0)[...].astype(f32)
    if joined:
        hidden_ref, own_ref, other_ref, gain_ref = refs[:4]
        refs = refs[4:]
        grad = grad + norm_back(
            hidden_ref[...].astype(f32), gain_ref[...], joined_sum(own_ref, other_ref)
        )
    gate_in, lift_in, gate_ref, up_ref, down_ref = refs[:5]
    refs = refs[5:]
    ffn_grad = grad.astype(bf16)
    if joined:
        refs.pop(0)[...] = grad
        refs.pop(0)[...] = ffn_grad
    grad_gate_out, grad_lift_out, partial_out = refs
    grad_inner = matmul(down_ref[...], ffn_grad, TN)
    gate = gate_in[...].astype(f32)
    lift = lift_in[...].astype(f32)
    sigmoid = jax.nn.sigmoid(gate)
    grad_gate = (grad_inner * lift * sigmoid * (1.0 + gate * (1.0 - sigmoid))).astype(bf16)
    grad_lift = (grad_inner * gate * sigmoid).astype(bf16)
    grad_gate_out[...] = grad_gate
    grad_lift_out[...] = grad_lift
    partial = matmul(gate_ref[...], grad_gate) + matmul(up_ref[...], grad_lift)
    partial_out[...] = partial.astype(bf16)


def call_ffn_backward(grad, joint, gate, lift, w_gate, w_up, w_down):
    features, length = grad.shape
    units = w_gate.shape[1]
    joined = joint is not None
    spec = functools.partial(token_spec, width=FFN_BLOCK)
    extra_in, extra_specs, extra_outs = [], [], []
    if joined:
        extra_in = list(joint)
        extra_specs = [spec(features)] * 3 + [full_spec(joint[3].shape)]
        extra_outs = [shape_of((features, length), f32), shape_of((features, length), bf16)]
    return pl.pallas_call(
        functools.partial(ffn_backward, joined),
        grid=(length // FFN_BLOCK,),
        in_specs=[spec(features)] + extra_specs + [spec(units)] * 2
        + [full_spec(a.shape) for a in (w_gate, w_up, w_down)],
        out_specs=[spec(features)] * len(extra_outs) + [spec(units)] * 2 + [spec(features)],
        out_shape=extra_outs + [shape_of((units, length), bf16)] * 2
        + [shape_of((features, length), bf16)],
        compiler_params=pltpu.CompilerParams(vmem_limit_bytes=40 * MIB),
        name="ffn_backward",
    )(grad, *extra_in, gate, lift, w_gate, w_up, w_down)


def attention_backward(slots, heads, segments, grad_ref, own_ref, other_ref, middle_ref, gain_ref,
                       wout_ref, wqkv_ref, attended_ref, query_ref, key_ref, turned_key_ref, value_ref,
                       cos_ref, sin_ref,
                       grad_out, attn_grad_out, projected_out, partial_out,
                       key_total, value_total, query_total, grad_heads, tri_ref):
    step = pl.num_programs(0) - 1 - pl.program_id(0)
    total = slots * heads
    half = HEAD // 2

    @pl.when(pl.program_id(0) == 0)
    def _():
        key_total[...] = jnp.zeros_like(key_total)
        value_total[...] = jnp.zeros_like(value_total)
        tri_ref[...] = causal_bias()

    grad = grad_ref[...].astype(f32)
    grad = grad + norm_back(middle_ref[...], gain_ref[...], joined_sum(own_ref, other_ref))
    grad_out[...] = grad
    attn_grad = grad.astype(bf16)
    attn_grad_out[...] = attn_grad
    grad_attended = matmul(wout_ref[...], attn_grad).astype(bf16)
    for h in range(total):
        s, j = divmod(h, heads)
        mine = grad_attended[h * HEAD : (h + 1) * HEAD]
        out = attended_ref[h * HEAD : (h + 1) * HEAD, :]
        delta = jnp.sum(mine.astype(f32) * out.astype(f32), axis=0, keepdims=True)
        lanes = slice(j * BLOCK, (j + 1) * BLOCK)
        grad_heads[s, :HEAD, lanes] = mine
        grad_heads[s, HEAD:, lanes] = jnp.concatenate(
            [part_rows(-delta, 0), jnp.zeros((LANES - HEAD - 8, BLOCK), f32)], axis=0
        ).astype(bf16)

    for s in range(slots):
        columns = slice(s * LANES, (s + 1) * LANES)
        features = slice(s * HEAD, (s + 1) * HEAD)

        def visit(back, s=s, columns=columns, features=features):
            keys = block_at(step - back)
            queries = jnp.concatenate(
                [query_ref[(s * heads + j) * LANES : (s * heads + j + 1) * LANES, :] for j in range(heads)],
                axis=1,
            )
            grads = grad_heads[s]
            scores = matmul(key_ref[keys, columns], queries)
            if back == 0:
                scores = scores + jnp.concatenate([tri_ref[...]] * heads, axis=1)
            weights = jnp.exp2(scores)
            value_total[features, keys] += matmul(grads[:HEAD], weights.astype(bf16), NT)
            grad_weights = matmul(value_ref[keys, columns], grads)
            grad_scores = (weights * grad_weights).astype(bf16)
            key_total[features, keys] += matmul(queries[:HEAD], grad_scores, NT)
            update = matmul(turned_key_ref[features, keys], grad_scores)
            if back == 0:
                query_total[s] = update
            else:
                query_total[s] += update

        visit(0)
        for back in (1, 2):
            pl.when(reaches(segments, step, back))(functools.partial(visit, back))

    cosine, sine = cos_ref[...], sin_ref[...]
    here = block_at(step)
    for h in range(total + 2 * slots):
        if h < total:
            s, j = divmod(h, heads)
            piece = query_total[s, :, j * BLOCK : (j + 1) * BLOCK] * (1.0 / math.sqrt(HEAD))
        elif h < total + slots:
            s = h - total
            piece = key_total[s * HEAD : (s + 1) * HEAD, here] * LN2
        else:
            s = h - total - slots
            piece = value_total[s * HEAD : (s + 1) * HEAD, here]
        if h < total + slots:
            upper, lower = turn(piece[:half], piece[half:], cosine, -sine)
            piece = jnp.concatenate([upper, lower], axis=0)
        projected_out[h * HEAD : (h + 1) * HEAD, :] = piece.astype(bf16)
    partial_out[...] = matmul(wqkv_ref[...], projected_out[...], TN).astype(bf16)


def call_attention_backward(segments, grad, own, other, middle, gain, wout, wqkv, attended, query, key,
                            turned_key, value, cosine, sine, slots, heads):
    features, length = middle.shape
    count = length // BLOCK

    def spec(rows):
        return pl.BlockSpec((rows, BLOCK), lambda i, *_: (0, count - 1 - i))

    return pl.pallas_call(
        functools.partial(attention_backward, slots, heads),
        grid_spec=pltpu.PrefetchScalarGridSpec(
            num_scalar_prefetch=1,
            grid=(count,),
            in_specs=[spec(features)] * 4
            + [full_spec(a.shape) for a in (gain, wout, wqkv)]
            + [spec(attended.shape[0]), spec(query.shape[0])]
            + [full_spec(a.shape) for a in (key, turned_key, value)]
            + [spec(HEAD // 2)] * 2,
            out_specs=[spec(features)] * 2 + [spec(wqkv.shape[0]), spec(features)],
            scratch_shapes=[
                pltpu.VMEM((slots * HEAD, length), f32),
                pltpu.VMEM((slots * HEAD, length), f32),
                pltpu.VMEM((slots, HEAD, heads * BLOCK), f32),
                pltpu.VMEM((slots, LANES, heads * BLOCK), bf16),
                pltpu.VMEM((BLOCK, BLOCK), f32),
            ],
        ),
        out_shape=[
            shape_of((features, length), f32), shape_of((features, length), bf16),
            shape_of((wqkv.shape[0], length), bf16), shape_of((features, length), bf16),
        ],
        compiler_params=pltpu.CompilerParams(vmem_limit_bytes=40 * MIB),
        name="attention_backward",
    )(segments, grad, own, other, middle, gain, wout, wqkv, attended, query, key, turned_key, value,
      cosine, sine)


def weight_grad(order, rows, count, *refs):
    lefts, rights = refs[:count], refs[count : 2 * count]
    out_ref = refs[2 * count]
    total = matmul(lefts[0][...], rights[0][...], NT)
    for number in range(1, count):
        total = total + matmul(lefts[number][...], rights[number][...], NT)
    width = total.shape[1]
    total = total.astype(out_ref.dtype)
    for place, shard in enumerate(order):
        out_ref[place, :rows, :width] = total[shard * rows : (shard + 1) * rows]
        if out_ref.shape[1] > rows:
            out_ref[place, rows:, :] = jnp.zeros(
                (out_ref.shape[1] - rows, out_ref.shape[2]), out_ref.dtype
            )
        if out_ref.shape[2] > width:
            out_ref[place, :rows, width:] = jnp.zeros(
                (rows, out_ref.shape[2] - width), out_ref.dtype
            )


def call_weight_grad(lefts, rights, order, width):
    features, length = lefts[0].shape
    columns = rights[0].shape[0]
    steps = -(-columns // width)
    size = len(order)
    rows = features // size
    padded = -(-rows // 16) * 16
    count = len(lefts)
    out_width = -(-width // LANES) * LANES
    return pl.pallas_call(
        functools.partial(weight_grad, order, rows, count),
        grid=(steps,),
        in_specs=[full_spec((features, length))] * count
        + [pl.BlockSpec((width, length), lambda i: (i, 0))] * count,
        out_specs=pl.BlockSpec((size, padded, out_width), lambda i: (0, 0, i)),
        out_shape=shape_of((size, padded, steps * out_width), bf16),
        compiler_params=pltpu.CompilerParams(vmem_limit_bytes=32 * MIB),
        name="weight_grad",
    )(*lefts, *rights)


def finish(grad_ref, hidden_ref, own_ref, other_ref, gain_ref, out_ref):
    out_ref[...] = grad_ref[...] + norm_back(
        hidden_ref[...].astype(f32), gain_ref[...], joined_sum(own_ref, other_ref)
    )


def call_finish(grad, hidden, own, other, gain):
    features, length = grad.shape
    return pl.pallas_call(
        finish,
        grid=(length // BLOCK,),
        in_specs=[token_spec(features)] * 4 + [full_spec(gain.shape)],
        out_specs=token_spec(features),
        out_shape=shape_of((features, length), f32),
        compiler_params=pltpu.CompilerParams(vmem_limit_bytes=32 * MIB),
        name="finish",
    )(grad, hidden, own, other, gain)


def gather_groups(owner, device, query_ref, key_ref, value_ref, out_ref, wqkv_out, wout_out):
    slot = pl.program_id(0)
    slots = pl.num_programs(0)
    _, held = group_of(slot, owner, device)
    group_cols, head = query_ref.shape[1], key_ref.shape[1]

    def place(first, height, piece):
        rows = pl.ds(pl.multiple_of(first, 16), height)
        return rows, jnp.where(held, piece, jnp.zeros_like(piece))

    rows, piece = place(slot * group_cols, group_cols, query_ref[0])
    wqkv_out[rows, :] = piece
    wout_out[rows, :] = place(slot * group_cols, group_cols, out_ref[0])[1]
    rows, piece = place(slots * group_cols + slot * head, head, key_ref[0])
    wqkv_out[rows, :] = piece
    rows, piece = place(slots * (group_cols + head) + slot * head, head, value_ref[0])
    wqkv_out[rows, :] = piece


def group_of(slot, owner, device):
    found, count = 0, 0
    for group in range(owner.shape[0]):
        mine = owner[group] == device[0]
        found = jnp.where(mine & (count == slot), group, found)
        count = count + jnp.where(mine, 1, 0)
    return found, count > slot


def call_gather_groups(owner, device, w_query, w_key, w_value, w_out, slots):
    features = w_query.shape[2]
    arrays = (w_query, w_key, w_value, w_out)
    joint = slots * (w_query.shape[1] + w_key.shape[1] + w_value.shape[1])
    outs = [(joint, features), (slots * w_out.shape[1], features)]
    return pl.pallas_call(
        gather_groups,
        grid_spec=pltpu.PrefetchScalarGridSpec(
            num_scalar_prefetch=2,
            grid=(slots,),
            in_specs=[
                pl.BlockSpec(
                    (1,) + a.shape[1:], lambda s, owner, device: (group_of(s, owner, device)[0], 0, 0)
                )
                for a in arrays
            ],
            out_specs=[out_full_spec(o) for o in outs],
        ),
        out_shape=[shape_of(o, bf16) for o in outs],
        name="gather_groups",
    )(owner, device, *arrays)


def rotary_tables(length):
    position = np.arange(length, dtype=np.float64)[None, :]
    column = np.arange(HEAD // 2, dtype=np.float64)[:, None]
    angles = position * np.exp(column * (-2.0 * math.log(10000.0) / HEAD))
    return jnp.asarray(np.cos(angles), f32), jnp.asarray(np.sin(angles), f32)


def exchange(own):
    return lax.ppermute(own, "mp", [(0, 1), (1, 0)])


def stage_plans(bit_count):
    if bit_count < 4:
        return [[[bit] for bit in range(bit_count)]] * 3
    tail = [[bit] for bit in range(4, bit_count)]
    return [
        [[0], [1], [2, 3]] + tail,
        [[1], [0], [2, 3]] + tail,
        [[2], [0], [1], [3]] + tail,
    ]


def shard_order(plan):
    bits = [bit for stage in plan for bit in stage]
    order = []
    for place in range(1 << len(bits)):
        shard = 0
        for rank, bit in enumerate(bits):
            if place >> (len(bits) - 1 - rank) & 1:
                shard |= 1 << bit
        order.append(shard)
    return order


def reduce_stage(current, stage, last):
    size = lax.axis_size("dp")
    index = lax.axis_index("dp")
    mine = 0
    for bit in stage:
        mine = mine * 2 + ((index >> bit) & 1)
    ways = 1 << len(stage)
    pieces = current.shape[0] // ways
    total = lax.dynamic_slice_in_dim(current, mine * pieces, pieces, 0).astype(f32)
    received = []
    for offset in range(1, ways):
        mask = 0
        for rank, bit in enumerate(stage):
            if offset >> (len(stage) - 1 - rank) & 1:
                mask |= 1 << bit
        outgoing = lax.dynamic_slice_in_dim(current, (mine ^ offset) * pieces, pieces, 0)
        received.append(lax.ppermute(outgoing, "dp", [(i, i ^ mask) for i in range(size)]))
    for piece in received:
        total = total + piece.astype(f32)
    return total if last else total.astype(bf16)


def reduce_scatter(payload, plan):
    for number, stage in enumerate(plan):
        payload = reduce_stage(payload, stage, number == len(plan) - 1)
    return payload[0]


def per_device(
    tokens_in,
    segment_ids,
    kv_owner,
    w_query,
    w_key,
    w_value,
    w_out,
    attn_gain,
    w_gate,
    w_up,
    w_down,
    ffn_gain,
    cotangent,
):
    features = tokens_in.shape[2]
    length = tokens_in.shape[1]
    group_cols = w_query.shape[2]
    heads = group_cols // HEAD
    slots = (kv_owner.shape[0] + lax.axis_size("mp") - 1) // lax.axis_size("mp")
    size = lax.axis_size("dp")
    rows = features // size

    device = lax.axis_index("mp").astype(jnp.int32)[None]
    wqkv, wout = call_gather_groups(
        kv_owner, device, *(jnp.swapaxes(w, 1, 2) for w in (w_query, w_key, w_value)), w_out, slots
    )
    w_down = w_down.T
    segments = segment_ids[0]
    cosine, sine = rotary_tables(length)
    gain_one, gain_two = (
        jnp.broadcast_to(gain.astype(f32)[:, None], (features, LANES)) for gain in (attn_gain, ffn_gain)
    )

    parts = (tokens_in[0].T,)
    saved = []
    for _ in range(REPEAT):
        outs = list(call_attention_forward(segments, parts, gain_one, wqkv, wout, cosine, sine, slots, heads))
        hidden = outs.pop(0) if len(parts) == 3 else parts[0]
        normed, query, key, turned_key, value, attended, partial = outs
        middle, normed_two, gate, lift, inner, partial_two = call_ffn_forward(
            hidden, partial, exchange(partial), gain_two, w_gate, w_up, w_down
        )
        parts = (middle, partial_two, exchange(partial_two))
        saved.append((hidden, normed, query, key, turned_key, value, attended, middle, normed_two, gate, lift, inner))
    tokens_out = (parts[0] + (parts[1].astype(f32) + parts[2].astype(f32))).astype(bf16)

    plans = stage_plans(size.bit_length() - 1)
    orders = [shard_order(plan) for plan in plans]
    joint = None
    grad = cotangent[0].T
    lefts, rights = [], []
    for r in reversed(range(REPEAT)):
        hidden, normed, query, key, turned_key, value, attended, middle, normed_two, gate, lift, inner = saved[r]
        outs = list(call_ffn_backward(grad, joint, gate, lift, w_gate, w_up, w_down))
        if joint is None:
            ffn_grad = grad
        else:
            grad = outs.pop(0)
            ffn_grad = outs.pop(0)
        grad_gate, grad_lift, partial = outs
        grad, attn_grad, projected, partial_two = call_attention_backward(
            segments, grad, partial, exchange(partial), middle, gain_two, wout, wqkv, attended, query,
            key, turned_key, value, cosine, sine, slots, heads,
        )
        joint = (hidden, partial_two, exchange(partial_two), gain_one)
        lefts.append((normed_two, ffn_grad, attn_grad, normed))
        rights.append((grad_gate, grad_lift, inner, attended, projected))
    grad_in = call_finish(grad, *joint)
    lefts = list(zip(*lefts))
    rights = list(zip(*rights))
    out_cols = slots * group_cols
    gate_total = reduce_scatter(call_weight_grad(lefts[0], rights[0], orders[0], 256), plans[0])
    up_total = reduce_scatter(call_weight_grad(lefts[0], rights[1], orders[1], 256), plans[1])
    down_total = reduce_scatter(call_weight_grad(lefts[1], rights[2], orders[2], 256), plans[2])
    out_total = reduce_scatter(call_weight_grad(lefts[2], rights[3], orders[1], out_cols), plans[1])
    qkv_total = reduce_scatter(
        call_weight_grad(lefts[3], rights[4], orders[0], wqkv.shape[0]), plans[0]
    )

    start = lax.axis_index("dp") * rows

    def my_rows(weights):
        return lax.dynamic_slice_in_dim(weights, start, rows, 0).astype(f32)

    gate_total, up_total, down_total, out_total, qkv_total = (
        total[:rows] for total in (gate_total, up_total, down_total, out_total, qkv_total)
    )
    qkv_total = qkv_total[:, : wqkv.shape[0]]
    wqkv_rows = lax.dynamic_slice_in_dim(wqkv, start, rows, 1).T.astype(f32)
    gains = jnp.stack([
        jnp.sum(qkv_total * wqkv_rows, axis=1),
        jnp.sum(gate_total * my_rows(w_gate) + up_total * my_rows(w_up), axis=1),
    ])
    gains = gains + exchange(gains)
    gains = gains / lax.dynamic_slice_in_dim(jnp.stack([attn_gain, ffn_gain]), start, rows, 1).astype(f32)

    def by_slot(array):
        return jnp.moveaxis(array.reshape(rows, slots, -1), 1, 0)

    key_start = slots * group_cols
    value_start = key_start + slots * HEAD
    return (
        tokens_out.T[None],
        grad_in.T[None],
        by_slot(qkv_total[:, :key_start]),
        by_slot(qkv_total[:, key_start:value_start]),
        by_slot(qkv_total[:, value_start:]),
        jnp.swapaxes(by_slot(out_total[:, :out_cols]), 1, 2),
        gate_total,
        up_total,
        down_total.T,
        gains[0],
        gains[1],
    )


def solution(mesh):
    in_specs = (
        P("dp", None, None),
        P("dp", None),
        P(),
        P(),
        P(),
        P(),
        P(),
        P(),
        P(None, "mp"),
        P(None, "mp"),
        P("mp", None),
        P(),
        P("dp", None, None),
    )
    out_specs = (
        P("dp", None, None),
        P("dp", None, None),
        P("mp", "dp", None),
        P("mp", "dp", None),
        P("mp", "dp", None),
        P("mp", None, "dp"),
        P("dp", "mp"),
        P("dp", "mp"),
        P("mp", "dp"),
        P("dp"),
        P("dp"),
    )
    return jax.shard_map(
        per_device, mesh=mesh, in_specs=in_specs, out_specs=out_specs, check_vma=False
    )
```

time: 811 us -> 430 us (0.53)
  matrix products: 372 us -> 0 us
  Pallas kernels: 0 us -> 214 us
  other arithmetic: 150 us -> 14.4 us
  local copies, waits for them, and re-layouts: 151 us -> 60.4 us
  loops' own time: 17.2 us -> 0 us
  waiting for transfers between devices: 70.2 us -> 85.9 us
  starting transfers between devices: 36.8 us -> 46 us
    dot_general x46 -> x0, matrix products: 284 us -> none  [the longest x4 49 us: backward_one_block(): jnp.einsum('sqjc,skc->sjqk', grad_block, values_all, preferred_element_ty...]
    pallas_call x0 -> x15, Pallas kernels: none -> 214 us  [the longest x2 52.1 us: call_attention_backward(): pl.pallas_call(functools.partial(attention_backward, slots, heads), grid_...]
    sub x8 -> x0, matrix products: 87.3 us -> none  [attend_block(): exponent = jnp.exp(scores - row_max)]
    convert_element_type x20 -> x11, other arithmetic: 67.2 us -> 3.73 us  [reduce_stage(): return total if last else total.astype(bf16)]
    reshape x10 -> x2, local copies, waits for them, and re-layouts: 23.5 us -> 0.27 us  [by_slot(): return jnp.moveaxis(array.reshape(rows, slots, -1), 1, 0)]
    reduce_sum x9 -> x2, other arithmetic: 25.4 us -> 3.28 us  [the longest x1 2.21 us: per_device(): jnp.sum(gate_total * my_rows(w_gate) + up_total * my_rows(w_up), axis=1)]
    dynamic_slice x24 -> x0, local copies, waits for them, and re-layouts: 21.2 us -> none  [the longest x4 10.4 us: backward_one_block(): grad_block = lax.dynamic_slice_in_dim(grad_attended, start, block_rows, 1)]
    add x15 -> x0, other arithmetic: 18.7 us -> none  [the longest x2 9.82 us: per_device(): grad_out + norm_back(middle, inverse_two, ffn_gain, grad_normed_two)]
  transfers between devices with their start and end apart: 32 -> 33, of which waited for: 12 -> 15; matrix products, arithmetic and copies ran while one was open for 34% -> 6% of each run, Pallas kernels for 0% -> 18%
where the time goes in v2:
time: 430 us; the launch traced here: 423 us
  Pallas kernels  214 us (50%)
  waiting for transfers between devices  85.9 us (20%)
  local copies, waits for them, and re-layouts  60.4 us (14%)
  starting transfers between devices  46 us (11%)
  other arithmetic  14.4 us (3%)
    ppermute x24, waiting for transfers between devices, reduce_stage(): lax.ppermute(outgoing, 'dp', [(i, i ^ mask) for i in range(size)])  70.2 us
    unnamed x166, local copies, waits for them, and re-layouts  52.5 us
    pallas_call x2, Pallas kernels, call_attention_backward(): pl.pallas_call(functools.partial(attention_backward, slots, heads), grid_...  52.1 us
    ppermute x24, starting transfers between devices, reduce_stage(): lax.ppermute(outgoing, 'dp', [(i, i ^ mask) for i in range(size)])  43.8 us
    pallas_call x2, Pallas kernels, call_attention_forward(): pl.pallas_call(functools.partial(attention_forward, joined, slots, heads)...  43.5 us
    pallas_call x2, Pallas kernels, call_ffn_forward(): pl.pallas_call(ffn_forward, grid=(length // FFN_BLOCK,), in_specs=[spec(f...  41 us
    pallas_call x2, Pallas kernels, call_ffn_backward(): pl.pallas_call(functools.partial(ffn_backward, joined), grid=(length // F...  39.8 us
    pallas_call x5, Pallas kernels, call_weight_grad(): pl.pallas_call(functools.partial(weight_grad, order, rows, count), grid=(...  26.6 us
  transfers between devices with their start and end apart: 33, of which 15 were waited for; matrix products, arithmetic and copies ran while one was open for 6% of the time, Pallas kernels for 18%

profile of v2, /device:TPU:0, one launch (start us, length us, event | category | flops | bytes accessed | tf_op | source)
XLA Modules:
  0.0 422.7 jit_solution(10895601409916752950)
XLA Ops:
  0.7 5.3 %gather_groups.1 = (bf16[960,960]{1,0:T(8,128)(2,1)}, bf16[576,960]{1,0:T(8,128)(2,1)}) custom-call(s32[5]{0:T(128)} %owner.1, s32[1]{0:T(128)} %bitcast.4.device, bf16[5,192,960]{2,1,0:T(8,128)(2,1)} %bitcast.65, bf16[5,64,960]{2,1,0:T(8,128)(2,1)} %bitcast.69, bf16[5,64,960]{2,1,0:T(8,128)(2,1)} %bitcast.70, bf16[5,192,960]{2,1,0:T(8,128)(2,1)} %out_ref.1), custom_call_target="tpu_custom_call" | custom-call | tf_op jit(solution)/shard_map/gather_groups/pallas_call | solution.py:533
  9.1 20.6 %attention_forward.2 = (bf16[960,1024]{1,0:T(8,128)(2,1)S(1)}, bf16[1152,1024]{1,0:T(8,128)(2,1)S(1)}, bf16[1024,384]{1,0:T(8,128)(2,1)S(1)}, bf16[192,1024]{1,0...) custom-call(s32[1024]{0:T(1024)S(1)} %bitcast.60, ...), custom_call_target="tpu_custom_call" | custom-call | tf_op jit(solution)/shard_map/attention_forward/pallas_call | solution.py:219
  40.3 21.0 %ffn_forward.2 = (f32[960,1024]{1,0:T(8,128)}, bf16[960,1024]{1,0:T(8,128)(2,1)S(1)}, bf16[1280,1024]{1,0:T(8,128)(2,1)}, bf16[1280,1024]{1,0:T(8,128)(2,1)}, bf...) custom-call(bf16[960,1024]{1,0:T(8,128)(2,1)S(1)} %bitcast.55, bf16[960,1024]{1,0:T(8,128)(2,1)S(1)} %get-tuple-element.58.own_ref, ...), custom_call_target="tpu_custom_call" | custom-call | tf_op jit(solution)/shard_map/ffn_forward/pallas_call | solution.py:259
  68.0 22.8 %attention_forward.3 = (f32[960,1024]{1,0:T(8,128)S(1)}, bf16[960,1024]{1,0:T(8,128)(2,1)S(1)}, bf16[1152,1024]{1,0:T(8,128)(2,1)S(1)}, bf16[1024,384]{1,0:T(8,1...) custom-call(s32[1024]{0:T(1024)S(1)} %bitcast.61, ...), custom_call_target="tpu_custom_call" | custom-call | tf_op jit(solution)/shard_map/attention_forward/pallas_call | solution.py:219
  103.7 20.1 %ffn_forward.3 = (f32[960,1024]{1,0:T(8,128)}, bf16[960,1024]{1,0:T(8,128)(2,1)S(1)}, bf16[1280,1024]{1,0:T(8,128)(2,1)}, bf16[1280,1024]{1,0:T(8,128)(2,1)}, bf...) custom-call(f32[960,1024]{1,0:T(8,128)} %copy-done.17, bf16[960,1024]{1,0:T(8,128)(2,1)S(1)} %copy-done.59, ...), custom_call_target="tpu_custom_call" | custom-call | tf_op jit(solution)/shard_map/ffn_forward/pallas_call | solution.py:259
  125.1 17.9 %ffn_backward.2 = (bf16[1280,1024]{1,0:T(8,128)(2,1)S(1)}, bf16[1280,1024]{1,0:T(8,128)(2,1)}, bf16[960,1024]{1,0:T(8,128)(2,1)S(1)}) custom-call(bf16[960,1024]{1,0:T(8,128)(2,1)S(1)} %bitcast.57, bf16[1280,1024]{1,0:T(8,128)(2,1)} %get-tuple-element.65.refs_1_, bf16[1280,1024]{1,0:T(8,128)(2,1)} %get-tuple-element.66.refs_2_, ...), custom_call_target="tpu_custom_call" | custom-call | tf_op jit(solution)/shard_map/ffn_backward/pallas_call | solution.py:310
  152.1 25.9 %attention_backward.2 = (f32[960,1024]{1,0:T(8,128)}, bf16[960,1024]{1,0:T(8,128)(2,1)S(1)}, bf16[960,1024]{1,0:T(8,128)(2,1)S(1)}, bf16[960,1024]{1,0:T(8,128)(2,1)}) custom-call(s32[1024]{0:T(1024)S(1)} %bitcast.62, bf16[960,1024]{1,0:T(8,128)(2,1)S(1)} %bitcast.58, bf16[960,1024]{1,0:T(8,128)(2,1)} %copy-done.62, bf16[960,1024]{1,0:T(8,128)(2,1)} %copy-done.78, ...), custom_call_target="tpu_custom_call" | custom-call | tf_op jit(solution)/shard_map/attention_backward/pallas_call | solution.py:411
  186.7 21.9 %ffn_backward.3 = (f32[960,1024]{1,0:T(8,128)}, bf16[960,1024]{1,0:T(8,128)(2,1)S(1)}, bf16[1280,1024]{1,0:T(8,128)(2,1)}, bf16[1280,1024]{1,0:T(8,128)(2,1)}, bf16[960,1024]{1,0:T(8,128)(2,1)S(1)}) custom-call(f32[960,1024]{1,0:T(8,128)} %get-tuple-element.73.refs_0_, f32[960,1024]{1,0:T(8,128)} %copy-done.17, bf16[960,1024]{1,0:T(8,128)(2,1)} %get-tuple-element.74.refs_2_, ...), custom_call_target="tpu_custom_call" | custom-call | tf_op jit(solution)/shard_map/ffn_backward/pallas_call | solution.py:310
  211.7 6.3 %weight_grad.8 = bf16[16,64,1280]{2,1,0:T(8,128)(2,1)S(1)} custom-call(bf16[960,1024]{1,0:T(8,128)(2,1)S(1)} %copy-done.24, bf16[960,1024]{1,0:T(8,128)(2,1)S(1)} %copy-done.21, bf16[1280,1024]{1,0:T(8,128)(2,1)S(1)} %copy-done.36, bf16[1280,1024]{1,0:T(8,128)(2,1)S(1)} %copy-done.37), custom_call_target="tpu_custom_call" | custom-call | tf_op jit(solution)/shard_map/weight_grad/pallas_call | solution.py:469
  220.7 11.5 %collective-permute-start.23 = (bf16[8,64,1280]{2,1,0:T(8,128)(2,1)}, bf16[8,64,1280]{2,1,0:T(8,128)(2,1)}, u32[]{:S(2)}, u32[]{:S(2)}) collective-permute-start(bf16[8,64,1280]{2,1,0:T(8,128)(2,1)} %constant_dynamic-slice_fusion.10), channel_id=1, source_target_pairs={{0,4},{2,6},{4,0},{6,2},{8,12},{10,14},{12,8},{14,10},{16,20},{18,... | collective-permute-start | bytes 3932168 | tf_op jit(solution)/shard_map/ppermute | solution.py:601
  241.3 6.5 %weight_grad.7 = bf16[16,64,1280]{2,1,0:T(8,128)(2,1)S(1)} custom-call(bf16[960,1024]{1,0:T(8,128)(2,1)S(1)} %copy-done.25, bf16[960,1024]{1,0:T(8,128)(2,1)S(1)} %copy-done.22, bf16[1280,1024]{1,0:T(8,128)(2,1)S(1)} %copy-done.34, bf16[1280,1024]{1,0:T(8,128)(2,1)S(1)} %copy-done.35), custom_call_target="tpu_custom_call" | custom-call | tf_op jit(solution)/shard_map/weight_grad/pallas_call | solution.py:469
  249.5 5.4 %fusion = bf16[1,1024,960]{1,2,0:T(8,128)(2,1)} fusion(f32[960,1024]{1,0:T(8,128)S(1)} %copy-done.76, bf16[960,1024]{1,0:T(8,128)(2,1)} %collective-permute-done.3, bf16[960,1024]{1,0:T(8,128)(2,1)} %get-tuple-element.64), kind=kLoop, calls=%fused_computation.5 | loop fusion | flops 4915200 | bytes 9830400 | tf_op jit(solution)/shard_map/broadcast_in_dim | solution.py:716
  254.9 6.3 %weight_grad.9 = bf16[16,64,1280]{2,1,0:T(8,128)(2,1)S(1)} custom-call(bf16[960,1024]{1,0:T(8,128)(2,1)S(1)} %bitcast.59, bf16[960,1024]{1,0:T(8,128)(2,1)S(1)} %copy-done.57, bf16[1280,1024]{1,0:T(8,128)(2,1)S(1)} %copy-done.32, bf16[1280,1024]{1,0:T(8,128)(2,1)S(1)} %copy-done.31), custom_call_target="tpu_custom_call" | custom-call | tf_op jit(solution)/shard_map/weight_grad/pallas_call | solution.py:469
  265.3 14.4 %collective-permute-done.18 = bf16[8,64,1280]{2,1,0:T(8,128)(2,1)S(1)} collective-permute-done((bf16[8,64,1280]{2,1,0:T(8,128)(2,1)S(1)}, bf16[8,64,1280]{2,1,0:T(8,128)(2,1)S(1)}, u32[]{:S(2)}, u32[]{:S(2)}) %collective-permute-start.18) | collective-permute-done | bytes 1310752 | tf_op jit(solution)/shard_map/ppermute | solution.py:601
  280.9 11.7 %collective-permute-done.28 = bf16[8,64,1280]{2,1,0:T(8,128)(2,1)S(1)} collective-permute-done((bf16[8,64,1280]{2,1,0:T(8,128)(2,1)S(1)}, bf16[8,64,1280]{2,1,0:T(8,128)(2,1)S(1)}, u32[]{:S(2)}, u32[]{:S(2)}) %collective-permute-start.28) | collective-permute-done | bytes 1310752 | tf_op jit(solution)/shard_map/ppermute | solution.py:601
  299.3 10.1 %collective-permute-done.29 = bf16[4,64,1280]{2,1,0:T(8,128)(2,1)S(1)} collective-permute-done((bf16[4,64,1280]{2,1,0:T(8,128)(2,1)S(1)}, bf16[4,64,1280]{2,1,0:T(8,128)(2,1)S(1)}, u32[]{:S(2)}, u32[]{:S(2)}) %collective-permute-start.29) | collective-permute-done | bytes 655392 | tf_op jit(solution)/shard_map/ppermute | solution.py:601
  314.7 26.2 %attention_backward.3 = (f32[960,1024]{1,0:T(8,128)}, bf16[960,1024]{1,0:T(8,128)(2,1)S(1)}, bf16[960,1024]{1,0:T(8,128)(2,1)S(1)}, bf16[960,1024]{1,0:T(8,128)(2,1)}) custom-call(s32[1024]{0:T(1024)S(1)} %bitcast.63, f32[960,1024]{1,0:T(8,128)} %get-tuple-element.77.grad_ref, bf16[960,1024]{1,0:T(8,128)(2,1)S(1)} %copy-done.55, ...), custom_call_target="tpu_custom_call" | custom-call | tf_op jit(solution)/shard_map/attention_backward/pallas_call | solution.py:411
  341.0 4.3 %weight_grad.5 = bf16[16,64,1024]{2,1,0:T(8,128)(2,1)S(1)} custom-call(bf16[960,1024]{1,0:T(8,128)(2,1)S(1)} %copy-done.49, bf16[960,1024]{1,0:T(8,128)(2,1)S(1)} %copy-done.47, bf16[960,1024]{1,0:T(8,128)(2,1)S(1)} %copy-done.51, bf16[960,1024]{1,0:T(8,128)(2,1)S(1)} %get-tuple-element.89.refs_3_), custom_call_target="tpu_custom_call" | custom-call | tf_op jit(solution)/shard_map/weight_grad/pallas_call | solution.py:469
  358.9 4.7 %collective-permute-done.30 = bf16[2,64,1280]{2,1,0:T(8,128)(2,1)S(1)} collective-permute-done((bf16[2,64,1280]{2,1,0:T(8,128)(2,1)S(1)}, bf16[2,64,1280]{2,1,0:T(8,128)(2,1)S(1)}, u32[]{:S(2)}, u32[]{:S(2)}) %collective-permute-start.30) | collective-permute-done | bytes 327712 | tf_op jit(solution)/shard_map/ppermute | solution.py:601
  365.7 9.8 %collective-permute-done.13 = bf16[8,64,640]{2,1,0:T(8,128)(2,1)S(1)} collective-permute-done((bf16[8,64,640]{2,1,0:T(8,128)(2,1)S(1)}, bf16[8,64,640]{2,1,0:T(8,128)(2,1)S(1)}, u32[]{:S(2)}, u32[]{:S(2)}) %collective-permute-start.13) | collective-permute-done | bytes 655392 | tf_op jit(solution)/shard_map/ppermute | solution.py:601
  377.1 4.1 collective-permute-done.8
  382.6 5.2 %collective-permute-done.14 = bf16[4,64,640]{2,1,0:T(8,128)(2,1)S(1)} collective-permute-done((bf16[4,64,640]{2,1,0:T(8,128)(2,1)S(1)}, bf16[4,64,640]{2,1,0:T(8,128)(2,1)S(1)}, u32[]{:S(2)}, u32[]{:S(2)}) %collective-permute-start.14) | collective-permute-done | bytes 327712 | tf_op jit(solution)/shard_map/ppermute | solution.py:601
  404.4 4.4 %collective-permute-done.10 = bf16[1,64,1024]{2,1,0:T(8,128)(2,1)} collective-permute-done((bf16[1,64,1024]{2,1,0:T(8,128)(2,1)}, bf16[1,64,1024]{2,1,0:T(8,128)(2,1)}, u32[]{:S(2)}, u32[]{:S(2)}) %collective-permute-start.10) | collective-permute-done | bytes 131104 | tf_op jit(solution)/shard_map/ppermute | solution.py:601
  416.5 5.7 %finish.1 = f32[960,1024]{1,0:T(8,128)} custom-call(f32[960,1024]{1,0:T(8,128)S(1)} %copy-done.30, bf16[960,1024]{1,0:T(8,128)(2,1)S(1)} %bitcast.56, bf16[960,1024]{1,0:T(8,128)(2,1)} %get-tuple-element.85.own_ref, bf16[960,1024]{1,0:T(8,128)(2,1)} %collective-permute-done.7.other_ref, f32[960,128]{1,0:T(8,128)S(1)} %broadcast_in_dim.10.refs_1_.refs_3_.refs_4_.gain_ref), custom_call_target="tpu_custom_call" | custom-call | tf_op jit(solution)/shard_map/finish/pallas_call | solution.py:489
  (270 shorter events, 128.6 us)
Async XLA Ops:
  181.1 68.4 %collective-permute-start.3 = (bf16[960,1024]{1,0:T(8,128)(2,1)}, bf16[960,1024]{1,0:T(8,128)(2,1)}, u32[]{:S(2)}, u32[]{:S(2)}) collective-permute-start(bf16[960,1024]{1,0:T(8,128)(2,1)} %get-tuple-element.64), channel_id=1, source_target_pairs={{0,1},{1,0},{2,3},{3,2},{4,5},{5,4},{6,7},{7,6},{8,9},{9,8},{10,11... | collective-permute-start | bytes 5898248 | tf_op jit(solution)/shard_map/ppermute | solution.py:559
  220.7 41.5 %collective-permute-start.23 = (bf16[8,64,1280]{2,1,0:T(8,128)(2,1)}, bf16[8,64,1280]{2,1,0:T(8,128)(2,1)}, u32[]{:S(2)}, u32[]{:S(2)}) collective-permute-start(bf16[8,64,1280]{2,1,0:T(8,128)(2,1)} %constant_dynamic-slice_fusion.10), channel_id=1, source_target_pairs={{0,4},{2,6},{4,0},{6,2},{8,12},{10,14},{12,8},{14,10},{16,20},{18,... | collective-permute-start | bytes 3932168 | tf_op jit(solution)/shard_map/ppermute | solution.py:601
  247.9 31.7 %collective-permute-start.18 = (bf16[8,64,1280]{2,1,0:T(8,128)(2,1)S(1)}, bf16[8,64,1280]{2,1,0:T(8,128)(2,1)S(1)}, u32[]{:S(2)}, u32[]{:S(2)}) collective-permute-start(bf16[8,64,1280]{2,1,0:T(8,128)(2,1)S(1)} %constant_dynamic-slice_fusion.15), channel_id=1, source_target_pairs={{0,2},{2,0},{4,6},{6,4},{8,10},{10,8},{12,14},{14,12},{16,18},{18,... | collective-permute-start | bytes 3932168 | tf_op jit(solution)/shard_map/ppermute | solution.py:601
  254.9 58.3 %collective-permute-start.6 = (bf16[960,1024]{1,0:T(8,128)(2,1)S(1)}, bf16[960,1024]{1,0:T(8,128)(2,1)S(1)}, u32[]{:S(2)}, u32[]{:S(2)}) collective-permute-start(bf16[960,1024]{1,0:T(8,128)(2,1)S(1)} %copy-done.55), channel_id=1, source_target_pairs={{0,1},{1,0},{2,3},{3,2},{4,5},{5,4},{6,7},{7,6},{8,9},{9,8},{10,11... | collective-permute-start | bytes 5898248 | tf_op jit(solution)/shard_map/ppermute | solution.py:559
  261.4 31.2 %collective-permute-start.28 = (bf16[8,64,1280]{2,1,0:T(8,128)(2,1)S(1)}, bf16[8,64,1280]{2,1,0:T(8,128)(2,1)S(1)}, u32[]{:S(2)}, u32[]{:S(2)}) collective-permute-start(bf16[8,64,1280]{2,1,0:T(8,128)(2,1)S(1)} %constant_dynamic-slice_fusion.5), channel_id=1, source_target_pairs={{0,8},{2,10},{4,12},{6,14},{8,0},{10,2},{12,4},{14,6},{16,24},{18,... | collective-permute-start | bytes 3932168 | tf_op jit(solution)/shard_map/ppermute | solution.py:601
  264.7 28.4 %collective-permute-start.24 = (bf16[4,64,1280]{2,1,0:T(8,128)(2,1)S(1)}, bf16[4,64,1280]{2,1,0:T(8,128)(2,1)S(1)}, u32[]{:S(2)}, u32[]{:S(2)}) collective-permute-start(bf16[4,64,1280]{2,1,0:T(8,128)(2,1)S(1)} %constant_dynamic-slice_fusion.9), channel_id=1, source_target_pairs={{0,2},{2,0},{4,6},{6,4},{8,10},{10,8},{12,14},{14,12},{16,18},{18,... | collective-permute-start | bytes 1966088 | tf_op jit(solution)/shard_map/ppermute | solution.py:601
  280.1 17.6 %collective-permute-start.19 = (bf16[4,64,1280]{2,1,0:T(8,128)(2,1)S(1)}, bf16[4,64,1280]{2,1,0:T(8,128)(2,1)S(1)}, u32[]{:S(2)}, u32[]{:S(2)}) collective-permute-start(bf16[4,64,1280]{2,1,0:T(8,128)(2,1)S(1)} %constant_dynamic-slice_fusion.14), channel_id=1, source_target_pairs={{0,4},{2,6},{4,0},{6,2},{8,12},{10,14},{12,8},{14,10},{16,20},{18,... | collective-permute-start | bytes 1966088 | tf_op jit(solution)/shard_map/ppermute | solution.py:601
  293.0 16.4 %collective-permute-start.29 = (bf16[4,64,1280]{2,1,0:T(8,128)(2,1)S(1)}, bf16[4,64,1280]{2,1,0:T(8,128)(2,1)S(1)}, u32[]{:S(2)}, u32[]{:S(2)}) collective-permute-start(bf16[4,64,1280]{2,1,0:T(8,128)(2,1)S(1)} %constant_dynamic-slice_fusion.4), channel_id=1, source_target_pairs={{0,2},{2,0},{4,6},{6,4},{8,10},{10,8},{12,14},{14,12},{16,18},{18,... | collective-permute-start | bytes 1966088 | tf_op jit(solution)/shard_map/ppermute | solution.py:601
  294.0 51.2 %collective-permute-start.27 = (bf16[1,64,1280]{2,1,0:T(8,128)(2,1)}, bf16[1,64,1280]{2,1,0:T(8,128)(2,1)S(1)}, u32[]{:S(2)}, u32[]{:S(2)}) collective-permute-start(bf16[1,64,1280]{2,1,0:T(8,128)(2,1)} %get-tuple-element.119), channel_id=1, source_target_pairs={{0,24},{2,26},{4,28},{6,30},{8,16},{10,18},{12,20},{14,22},{16,8},... | collective-permute-start | bytes 491528 | tf_op jit(solution)/shard_map/ppermute | solution.py:601
  297.6 54.8 %collective-permute-start.26 = (bf16[1,64,1280]{2,1,0:T(8,128)(2,1)S(1)}, bf16[1,64,1280]{2,1,0:T(8,128)(2,1)S(1)}, u32[]{:S(2)}, u32[]{:S(2)}) collective-permute-start(bf16[1,64,1280]{2,1,0:T(8,128)(2,1)S(1)} %get-tuple-element.120), channel_id=1, source_target_pairs={{0,8},{2,10},{4,12},{6,14},{8,0},{10,2},{12,4},{14,6},{16,24},{18,... | collective-permute-start | bytes 491528 | tf_op jit(solution)/shard_map/ppermute | solution.py:601
  297.7 57.4 %collective-permute-start.25 = (bf16[1,64,1280]{2,1,0:T(8,128)(2,1)S(1)}, bf16[1,64,1280]{2,1,0:T(8,128)(2,1)S(1)}, u32[]{:S(2)}, u32[]{:S(2)}) collective-permute-start(bf16[1,64,1280]{2,1,0:T(8,128)(2,1)S(1)} %get-tuple-element.118), channel_id=1, source_target_pairs={{0,16},{2,18},{4,20},{6,22},{8,24},{10,26},{12,28},{14,30},{16,0},... | collective-permute-start | bytes 491528 | tf_op jit(solution)/shard_map/ppermute | solution.py:601
  309.4 45.8 %collective-permute-start.22 = (bf16[1,64,1280]{2,1,0:T(8,128)(2,1)}, bf16[1,64,1280]{2,1,0:T(8,128)(2,1)S(1)}, u32[]{:S(2)}, u32[]{:S(2)}) collective-permute-start(bf16[1,64,1280]{2,1,0:T(8,128)(2,1)} %get-tuple-element.116), channel_id=1, source_target_pairs={{0,24},{2,26},{4,28},{6,30},{8,16},{10,18},{12,20},{14,22},{16,8},... | collective-permute-start | bytes 491528 | tf_op jit(solution)/shard_map/ppermute | solution.py:601
  313.2 42.3 %collective-permute-start.21 = (bf16[1,64,1280]{2,1,0:T(8,128)(2,1)S(1)}, bf16[1,64,1280]{2,1,0:T(8,128)(2,1)S(1)}, u32[]{:S(2)}, u32[]{:S(2)}) collective-permute-start(bf16[1,64,1280]{2,1,0:T(8,128)(2,1)S(1)} %get-tuple-element.117), channel_id=1, source_target_pairs={{0,8},{2,10},{4,12},{6,14},{8,0},{10,2},{12,4},{14,6},{16,24},{18,... | collective-permute-start | bytes 491528 | tf_op jit(solution)/shard_map/ppermute | solution.py:601
  345.3 11.5 %collective-permute-start.20 = (bf16[1,64,1280]{2,1,0:T(8,128)(2,1)S(1)}, bf16[1,64,1280]{2,1,0:T(8,128)(2,1)S(1)}, u32[]{:S(2)}, u32[]{:S(2)}) collective-permute-start(bf16[1,64,1280]{2,1,0:T(8,128)(2,1)S(1)} %get-tuple-element.115), channel_id=1, source_target_pairs={{0,16},{2,18},{4,20},{6,22},{8,24},{10,26},{12,28},{14,30},{16,0},... | collective-permute-start | bytes 491528 | tf_op jit(solution)/shard_map/ppermute | solution.py:601
  352.5 11.2 %collective-permute-start.30 = (bf16[2,64,1280]{2,1,0:T(8,128)(2,1)S(1)}, bf16[2,64,1280]{2,1,0:T(8,128)(2,1)S(1)}, u32[]{:S(2)}, u32[]{:S(2)}) collective-permute-start(bf16[2,64,1280]{2,1,0:T(8,128)(2,1)S(1)} %constant_dynamic-slice_fusion.3), channel_id=1, source_target_pairs={{0,4},{2,6},{4,0},{6,2},{8,12},{10,14},{12,8},{14,10},{16,20},{18,... | collective-permute-start | bytes 983048 | tf_op jit(solution)/shard_map/ppermute | solution.py:601
  355.1 59.3 %collective-permute-start.7 = (bf16[960,1024]{1,0:T(8,128)(2,1)}, bf16[960,1024]{1,0:T(8,128)(2,1)}, u32[]{:S(2)}, u32[]{:S(2)}) collective-permute-start(bf16[960,1024]{1,0:T(8,128)(2,1)} %get-tuple-element.85.own_ref), channel_id=1, source_target_pairs={{0,1},{1,0},{2,3},{3,2},{4,5},{5,4},{6,7},{7,6},{8,9},{9,8},{10,11... | collective-permute-start | bytes 5898248 | tf_op jit(solution)/shard_map/ppermute | solution.py:559
  355.2 26.0 %collective-permute-start.8 = (bf16[8,64,1024]{2,1,0:T(8,128)(2,1)S(1)}, bf16[8,64,1024]{2,1,0:T(8,128)(2,1)S(1)}, u32[]{:S(2)}, u32[]{:S(2)}) collective-permute-start(bf16[8,64,1024]{2,1,0:T(8,128)(2,1)S(1)} %constant_dynamic-slice_fusion.25), channel_id=1, source_target_pairs={{0,2},{2,0},{4,6},{6,4},{8,10},{10,8},{12,14},{14,12},{16,18},{18,... | collective-permute-start | bytes 3145736 | tf_op jit(solution)/shard_map/ppermute | solution.py:601
  355.5 19.9 %collective-permute-start.13 = (bf16[8,64,640]{2,1,0:T(8,128)(2,1)S(1)}, bf16[8,64,640]{2,1,0:T(8,128)(2,1)S(1)}, u32[]{:S(2)}, u32[]{:S(2)}) collective-permute-start(bf16[8,64,640]{2,1,0:T(8,128)(2,1)S(1)} %constant_dynamic-slice_fusion.20), channel_id=1, source_target_pairs={{0,4},{2,6},{4,0},{6,2},{8,12},{10,14},{12,8},{14,10},{16,20},{18,... | collective-permute-start | bytes 1966088 | tf_op jit(solution)/shard_map/ppermute | solution.py:601
  363.8 18.0 %collective-permute-start.31 = (bf16[1,64,1280]{2,1,0:T(8,128)(2,1)S(1)}, bf16[1,64,1280]{2,1,0:T(8,128)(2,1)S(1)}, u32[]{:S(2)}, u32[]{:S(2)}) collective-permute-start(bf16[1,64,1280]{2,1,0:T(8,128)(2,1)S(1)} %constant_dynamic-slice_fusion.1), channel_id=1, source_target_pairs={{0,16},{2,18},{4,20},{6,22},{8,24},{10,26},{12,28},{14,30},{16,0},... | collective-permute-start | bytes 491528 | tf_op jit(solution)/shard_map/ppermute | solution.py:601
  375.7 12.1 %collective-permute-start.14 = (bf16[4,64,640]{2,1,0:T(8,128)(2,1)S(1)}, bf16[4,64,640]{2,1,0:T(8,128)(2,1)S(1)}, u32[]{:S(2)}, u32[]{:S(2)}) collective-permute-start(bf16[4,64,640]{2,1,0:T(8,128)(2,1)S(1)} %constant_dynamic-slice_fusion.19), channel_id=1, source_target_pairs={{0,2},{2,0},{4,6},{6,4},{8,10},{10,8},{12,14},{14,12},{16,18},{18,... | collective-permute-start | bytes 983048 | tf_op jit(solution)/shard_map/ppermute | solution.py:601
  381.7 13.1 %collective-permute-start.9 = (bf16[4,64,1024]{2,1,0:T(8,128)(2,1)S(1)}, bf16[4,64,1024]{2,1,0:T(8,128)(2,1)S(1)}, u32[]{:S(2)}, u32[]{:S(2)}) collective-permute-start(bf16[4,64,1024]{2,1,0:T(8,128)(2,1)S(1)} %constant_dynamic-slice_fusion.24), channel_id=1, source_target_pairs={{0,4},{2,6},{4,0},{6,2},{8,12},{10,14},{12,8},{14,10},{16,20},{18,... | collective-permute-start | bytes 1572872 | tf_op jit(solution)/shard_map/ppermute | solution.py:601
  388.5 9.7 %collective-permute-start.16 = (bf16[1,64,640]{2,1,0:T(8,128)(2,1)S(1)}, bf16[1,64,640]{2,1,0:T(8,128)(2,1)S(1)}, u32[]{:S(2)}, u32[]{:S(2)}) collective-permute-start(bf16[1,64,640]{2,1,0:T(8,128)(2,1)S(1)} %get-tuple-element.126), channel_id=1, source_target_pairs={{0,8},{2,10},{4,12},{6,14},{8,0},{10,2},{12,4},{14,6},{16,24},{18,... | collective-permute-start | bytes 245768 | tf_op jit(solution)/shard_map/ppermute | solution.py:601
  390.4 9.8 %collective-permute-start.15 = (bf16[1,64,640]{2,1,0:T(8,128)(2,1)S(1)}, bf16[1,64,640]{2,1,0:T(8,128)(2,1)S(1)}, u32[]{:S(2)}, u32[]{:S(2)}) collective-permute-start(bf16[1,64,640]{2,1,0:T(8,128)(2,1)S(1)} %get-tuple-element.124), channel_id=1, source_target_pairs={{0,16},{2,18},{4,20},{6,22},{8,24},{10,26},{12,28},{14,30},{16,0},... | collective-permute-start | bytes 245768 | tf_op jit(solution)/shard_map/ppermute | solution.py:601
  398.2 10.7 %collective-permute-start.10 = (bf16[1,64,1024]{2,1,0:T(8,128)(2,1)}, bf16[1,64,1024]{2,1,0:T(8,128)(2,1)}, u32[]{:S(2)}, u32[]{:S(2)}) collective-permute-start(bf16[1,64,1024]{2,1,0:T(8,128)(2,1)} %get-tuple-element.121), channel_id=1, source_target_pairs={{0,16},{2,18},{4,20},{6,22},{8,24},{10,26},{12,28},{14,30},{16,0},... | collective-permute-start | bytes 393224 | tf_op jit(solution)/shard_map/ppermute | solution.py:601
  (90 other events, 894.0 us)
